TPU v7x, 32 devices: a whole 2x2x4 slice. The times are simulated.
32 devices in a mesh: gr: 4 (over y, x), gc: 8 (over z, core).
Axes of the slice: x: 2, y: 2, z: 4, core: 2. Of those that a mesh axis runs over, the one named last changes fastest.
Arguments:
- jacobian: bfloat16 [65536, 1536], P(('gr', 'gc')), may hold values from -0.43164062 to 0.43164062
- class_scores: float32 [192, 8], replicated, may hold values from 0.1 to 10
- source: int32 [32768], replicated, may hold values from 0 to 65535, as said below
Outputs:
- gram_slab: float32 [2048, 32768], P('gr', 'gc')
Inputs may be any that keep to these rules, and one draw needn't show every extreme that they name: `source`: entries are distinct. Entry k is o * 2048 + j for owner o (flat index over gr then gc) and local column j. In each aligned tile of 4096 consecutive entries no owner appears more than 192 times, and some owner appears exactly 192 times in every tile.
All inputs are finite; a program needn't handle non-finite values.
Results may differ from a plain program's by a relative error of at most 0.0033.
Values may be sent and summed in bfloat16 or wider, within the bound.
A program may use at most 128 MiB of HBM per device.

v0:
```python
import jax
import jax.numpy as jnp
from jax import lax
from jax.sharding import PartitionSpec as P

SLAB_DEV = 512


def broadcast(x, axis, root):
    mine = lax.axis_index(axis) == root
    return lax.psum(jnp.where(mine, x, jnp.zeros_like(x)), axis)


def weigh_rows(block, probs, root):
    values = block.astype(jnp.float32).reshape(block.shape[0], probs.shape[0], probs.shape[1])
    centre = jnp.sum(values * probs, axis=-1, keepdims=True)
    return (root * (values - centre)).astype(jnp.bfloat16).reshape(block.shape[0], -1)


def local(jacobian, class_scores, source):
    count_rows = lax.axis_size("gr")
    count_cols = lax.axis_size("gc")
    grid_row = lax.axis_index("gr")
    grid_col = lax.axis_index("gc")
    myself = grid_row * count_cols + grid_col
    local_width = jacobian.shape[0]
    all_rows = jacobian.shape[1]
    total_weights = source.shape[0]
    tile_width = total_weights // count_cols
    capacity = 3 * (total_weights // (count_cols * count_cols * count_rows)) // 2
    token_count = class_scores.shape[0]
    block_rows = all_rows // count_rows
    block_tokens = token_count // count_rows
    probs = class_scores / jnp.sum(class_scores, axis=1, keepdims=True)
    root = jnp.sqrt(probs)
    owners = (source // local_width).reshape(count_cols, tile_width)
    locals_all = (source % local_width).reshape(count_cols, tile_width)
    owned = owners == myself
    owned_count = jnp.cumsum(owned.astype(jnp.int32), axis=1)
    targets = jnp.arange(1, capacity + 1, dtype=jnp.int32)
    found_at = jax.vmap(lambda row: jnp.searchsorted(row, targets, side="left"))(owned_count)
    found_at = jnp.minimum(found_at, tile_width - 1)
    send_index = jnp.take_along_axis(locals_all, found_at, axis=1)
    send_used = targets[None, :] <= owned_count[:, -1:]
    picked = jnp.take(jacobian, send_index.reshape(-1), axis=0)
    picked = jnp.where(send_used.reshape(-1)[:, None], picked, jnp.zeros_like(picked))
    tile_source = (
        lax.dynamic_slice_in_dim(source, grid_col * tile_width, tile_width, 0) // local_width
    )
    onehot = (
        tile_source[:, None] == jnp.arange(count_rows * count_cols, dtype=jnp.int32)[None, :]
    ).astype(jnp.int32)
    arrival = jnp.sum(jnp.cumsum(onehot, axis=0) * onehot, axis=1) - 1
    source_row = tile_source // count_cols
    source_col = tile_source % count_cols
    outgoing = picked.reshape(count_cols, capacity, count_rows, block_rows)
    incoming = lax.all_to_all(
        lax.all_to_all(outgoing, "gr", split_axis=2, concat_axis=2, tiled=True),
        "gc",
        split_axis=0,
        concat_axis=0,
        tiled=True,
    )
    flat_index = source_col * capacity * count_rows + arrival * count_rows + source_row
    tile_block = jnp.take(incoming.reshape(-1, block_rows), flat_index, axis=0)
    probs_block = lax.dynamic_slice_in_dim(probs, grid_row * block_tokens, block_tokens, 0)
    root_block = lax.dynamic_slice_in_dim(root, grid_row * block_tokens, block_tokens, 0)
    tile_block = weigh_rows(tile_block, probs_block, root_block)
    full_tile = lax.all_gather(tile_block, "gr", axis=1, tiled=True)
    slab_total = SLAB_DEV * count_rows
    slab_piece = lax.dynamic_slice_in_dim(
        full_tile, tile_width - slab_total + grid_row * SLAB_DEV, SLAB_DEV, 0
    )
    slab_part = broadcast(slab_piece, "gc", count_cols - 1)
    product = lax.dot_general(
        slab_part, full_tile, (((1,), (1,)), ((), ())), preferred_element_type=jnp.float32
    )
    positions = (
        total_weights - slab_total + grid_row * SLAB_DEV + jnp.arange(SLAB_DEV, dtype=jnp.int32)
    )
    column_ids = grid_col * tile_width + jnp.arange(tile_width, dtype=jnp.int32)
    return jnp.where(column_ids[None, :] <= positions[:, None], product, jnp.float32(0.0))


def solution(mesh):
    in_specs = (P(("gr", "gc"), None), P(), P())
    out_specs = P("gr", "gc")
    return jax.shard_map(local, mesh=mesh, in_specs=in_specs, out_specs=out_specs, check_vma=False)
```

profile of v0, /device:TPU:1, one launch (start us, length us, event | category | flops | bytes accessed | tf_op | source)
XLA Modules:
  0.0 607.9 jit_solution(10764516535468649334)
XLA Ops:
  11.7 131.5 %while.24 = (s32[]{:T(128)}, u32[8,192]{1,0:T(8,128)S(1)}, u32[8,192]{1,0:T(8,128)S(1)}, s32[8,4096]{1,0:T(8,128)S(1)}, s32[]{:T(128)}, /*index=5*/s32[]{:T(128)}) while((s32[]{:T(128)}, u32[8,192]{1,0:T(8,128)S(1)}, u32[8,192]{1,0:T(8,128)S(1)}, s32[8,4096]{1,0:T(8,128)S(1)}, s32[]{:T(128)}, /*index=5*/s32[]{:T(128)}) %tuple.44), condition=%wide.region_7.8_spmd.clone, body=%wide.region_6.7_spmd.clone.sunk | while | flops 35523 | bytes 127569 | solution.py:41
  11.8 9.9 %gather_fusion = s32[1536]{0:T(1024)S(1)} fusion(s32[8,4096]{1,0:T(8,128)S(1)} %get-tuple-element.149, u32[1536]{0:T(1024)S(1)} %reshape.203), kind=kCustom, calls=%fused_computation.clone.clone.1 | custom fusion | bytes 24576 | tf_op jit(solution)/shard_map/vmap(jit(searchsorted))/vmap(jit(_searchsorted_scan_impl))/while/body/eval_jaxpr/gather | solution.py:41
  21.9 9.9 %gather_fusion = s32[1536]{0:T(1024)S(1)} fusion(s32[8,4096]{1,0:T(8,128)S(1)} %get-tuple-element.149, u32[1536]{0:T(1024)S(1)} %reshape.203), kind=kCustom, calls=%fused_computation.clone.clone.1 | custom fusion | bytes 24576 | tf_op jit(solution)/shard_map/vmap(jit(searchsorted))/vmap(jit(_searchsorted_scan_impl))/while/body/eval_jaxpr/gather | solution.py:41
  32.0 9.9 %gather_fusion = s32[1536]{0:T(1024)S(1)} fusion(s32[8,4096]{1,0:T(8,128)S(1)} %get-tuple-element.149, u32[1536]{0:T(1024)S(1)} %reshape.203), kind=kCustom, calls=%fused_computation.clone.clone.1 | custom fusion | bytes 24576 | tf_op jit(solution)/shard_map/vmap(jit(searchsorted))/vmap(jit(_searchsorted_scan_impl))/while/body/eval_jaxpr/gather | solution.py:41
  42.1 9.9 %gather_fusion = s32[1536]{0:T(1024)S(1)} fusion(s32[8,4096]{1,0:T(8,128)S(1)} %get-tuple-element.149, u32[1536]{0:T(1024)S(1)} %reshape.203), kind=kCustom, calls=%fused_computation.clone.clone.1 | custom fusion | bytes 24576 | tf_op jit(solution)/shard_map/vmap(jit(searchsorted))/vmap(jit(_searchsorted_scan_impl))/while/body/eval_jaxpr/gather | solution.py:41
  52.3 9.9 %gather_fusion = s32[1536]{0:T(1024)S(1)} fusion(s32[8,4096]{1,0:T(8,128)S(1)} %get-tuple-element.149, u32[1536]{0:T(1024)S(1)} %reshape.203), kind=kCustom, calls=%fused_computation.clone.clone.1 | custom fusion | bytes 24576 | tf_op jit(solution)/shard_map/vmap(jit(searchsorted))/vmap(jit(_searchsorted_scan_impl))/while/body/eval_jaxpr/gather | solution.py:41
  62.4 9.9 %gather_fusion = s32[1536]{0:T(1024)S(1)} fusion(s32[8,4096]{1,0:T(8,128)S(1)} %get-tuple-element.149, u32[1536]{0:T(1024)S(1)} %reshape.203), kind=kCustom, calls=%fused_computation.clone.clone.1 | custom fusion | bytes 24576 | tf_op jit(solution)/shard_map/vmap(jit(searchsorted))/vmap(jit(_searchsorted_scan_impl))/while/body/eval_jaxpr/gather | solution.py:41
  72.5 9.9 %gather_fusion = s32[1536]{0:T(1024)S(1)} fusion(s32[8,4096]{1,0:T(8,128)S(1)} %get-tuple-element.149, u32[1536]{0:T(1024)S(1)} %reshape.203), kind=kCustom, calls=%fused_computation.clone.clone.1 | custom fusion | bytes 24576 | tf_op jit(solution)/shard_map/vmap(jit(searchsorted))/vmap(jit(_searchsorted_scan_impl))/while/body/eval_jaxpr/gather | solution.py:41
  82.6 9.9 %gather_fusion = s32[1536]{0:T(1024)S(1)} fusion(s32[8,4096]{1,0:T(8,128)S(1)} %get-tuple-element.149, u32[1536]{0:T(1024)S(1)} %reshape.203), kind=kCustom, calls=%fused_computation.clone.clone.1 | custom fusion | bytes 24576 | tf_op jit(solution)/shard_map/vmap(jit(searchsorted))/vmap(jit(_searchsorted_scan_impl))/while/body/eval_jaxpr/gather | solution.py:41
  92.7 9.9 %gather_fusion = s32[1536]{0:T(1024)S(1)} fusion(s32[8,4096]{1,0:T(8,128)S(1)} %get-tuple-element.149, u32[1536]{0:T(1024)S(1)} %reshape.203), kind=kCustom, calls=%fused_computation.clone.clone.1 | custom fusion | bytes 24576 | tf_op jit(solution)/shard_map/vmap(jit(searchsorted))/vmap(jit(_searchsorted_scan_impl))/while/body/eval_jaxpr/gather | solution.py:41
  102.8 9.9 %gather_fusion = s32[1536]{0:T(1024)S(1)} fusion(s32[8,4096]{1,0:T(8,128)S(1)} %get-tuple-element.149, u32[1536]{0:T(1024)S(1)} %reshape.203), kind=kCustom, calls=%fused_computation.clone.clone.1 | custom fusion | bytes 24576 | tf_op jit(solution)/shard_map/vmap(jit(searchsorted))/vmap(jit(_searchsorted_scan_impl))/while/body/eval_jaxpr/gather | solution.py:41
  112.9 9.9 %gather_fusion = s32[1536]{0:T(1024)S(1)} fusion(s32[8,4096]{1,0:T(8,128)S(1)} %get-tuple-element.149, u32[1536]{0:T(1024)S(1)} %reshape.203), kind=kCustom, calls=%fused_computation.clone.clone.1 | custom fusion | bytes 24576 | tf_op jit(solution)/shard_map/vmap(jit(searchsorted))/vmap(jit(_searchsorted_scan_impl))/while/body/eval_jaxpr/gather | solution.py:41
  123.0 9.9 %gather_fusion = s32[1536]{0:T(1024)S(1)} fusion(s32[8,4096]{1,0:T(8,128)S(1)} %get-tuple-element.149, u32[1536]{0:T(1024)S(1)} %reshape.203), kind=kCustom, calls=%fused_computation.clone.clone.1 | custom fusion | bytes 24576 | tf_op jit(solution)/shard_map/vmap(jit(searchsorted))/vmap(jit(_searchsorted_scan_impl))/while/body/eval_jaxpr/gather | solution.py:41
  133.2 9.9 %gather_fusion = s32[1536]{0:T(1024)S(1)} fusion(s32[8,4096]{1,0:T(8,128)S(1)} %get-tuple-element.149, u32[1536]{0:T(1024)S(1)} %reshape.203), kind=kCustom, calls=%fused_computation.clone.clone.1 | custom fusion | bytes 24576 | tf_op jit(solution)/shard_map/vmap(jit(searchsorted))/vmap(jit(_searchsorted_scan_impl))/while/body/eval_jaxpr/gather | solution.py:41
  143.3 9.9 %gather_fusion.3 = s32[1536]{0:T(1024)S(1)} fusion(s32[8,4096]{1,0:T(8,128)S(1)} %reshape.144, s32[1536]{0:T(1024)S(1)} %reshape.171), kind=kCustom, calls=%fused_computation.3 | custom fusion | bytes 24576 | tf_op jit(solution)/shard_map/jit(take_along_axis)/gather | solution.py:43
  153.5 14.0 %gather_fusion.1 = bf16[1536,1536]{1,0:T(8,128)(2,1)} fusion(bf16[2048,1536]{1,0:T(8,128)(2,1)} %param.5, s32[2048]{0:T(1024)S(1)} %pad_clamp_fusion), kind=kCustom, calls=%fused_computation.1 | custom fusion | bytes 9443328 | tf_op jit(solution)/shard_map/jit(_take)/gather | solution.py:45
  167.4 9.0 %gather.24 = bf16[8,192,4,384]{3,2,1,0:T(4,128)(2,1)} reshape(bf16[1536,1536]{1,0:T(8,128)(2,1)} %gather_fusion.1) | data formatting | bytes 9437184 | tf_op jit(solution)/shard_map/jit(_take)/gather | solution.py:45
  176.5 4.2 fusion.8
  180.7 56.3 %all_to_all.10 = bf16[8,192,4,384]{3,1,0,2:T(8,128)(2,1)S(1)} all-to-all(bf16[8,192,4,384]{3,1,0,2:T(8,128)(2,1)S(1)} %fusion.8), channel_id=1, replica_groups=mesh['gr'=4,'gc'=8] {'gr'}, dimensions={2} | all-to-all | bytes 9437184 | tf_op jit(solution)/shard_map/all_to_all | solution.py:58
  239.7 7.2 %all-to-all-start.1 = ((bf16[8,192,4,384]{3,1,2,0:T(8,128)(2,1)}), bf16[8,192,4,384]{3,1,2,0:T(8,128)(2,1)}, u32[]{:S(2)}, u32[]{:S(2)}) async-start(bf16[8,192,4,384]{3,1,2,0:T(8,128)(2,1)} %copy.17), calls=%async_computation.1 | async-start | bytes 9437184 | tf_op jit(solution)/shard_map/all_to_all | solution.py:57
  248.1 9.2 %reduce-window.14 = s32[32,32,128]{2,1,0:T(8,128)S(1)} reduce-window(s32[32,32,128]{2,1,0:T(8,128)S(1)} %fusion.13, s32[]{:T(128)} %constant.155.clone.1), window={size=1x1x128 pad=0_0x0_0x127_0}, to_apply=%region_1.2 | reduce-window | flops 16646144 | bytes 1048580 | tf_op jit(solution)/shard_map/reduce-window
  260.3 91.0 %all-to-all-done.1 = bf16[8,192,4,384]{3,1,2,0:T(8,128)(2,1)} async-done(((bf16[8,192,4,384]{3,1,2,0:T(8,128)(2,1)}), bf16[8,192,4,384]{3,1,2,0:T(8,128)(2,1)}, u32[]{:S(2)}, u32[]{:S(2)}) %all-to-all-start.1) | async-done | bytes 4718624 | tf_op jit(solution)/shard_map/all_to_all | solution.py:57
  351.4 8.2 %copy.18 = bf16[8,192,4,384]{3,2,1,0:T(4,128)(2,1)} copy(bf16[8,192,4,384]{3,1,2,0:T(8,128)(2,1)} %all-to-all-done.1) | data formatting | bytes 9437184 | tf_op jit(solution)/shard_map/all_to_all | solution.py:57
  359.5 8.5 %reshape.146 = bf16[6144,384]{1,0:T(8,128)(2,1)} reshape(bf16[8,192,4,384]{3,2,1,0:T(4,128)(2,1)} %copy.18) | data formatting | bytes 9437184 | tf_op jit(solution)/shard_map/reshape | solution.py:65
  368.1 17.0 %gather_fusion.2 = bf16[4096,384]{1,0:T(8,128)(2,1)S(1)} fusion(bf16[6144,384]{1,0:T(8,128)(2,1)} %reshape.146, s32[4096]{0:T(1024)S(1)} %broadcast_clamp_fusion), kind=kCustom, calls=%fused_computation.2 | custom fusion | bytes 6307840 | tf_op jit(solution)/shard_map/jit(_take)/gather | solution.py:65
  385.1 2.9 copy.19
  388.0 6.6 %fusion.5 = f32[4096,384]{0,1:T(8,128)} fusion(f32[48,8]{1,0:T(8,128)S(1)} %copy.20, bf16[4096,384]{0,1:T(8,128)(2,1)} %copy.19, pred[4096]{0:T(1024)(128)(4,1)S(1)} %get-tuple-element.100), kind=kOutput, calls=%fused_computation.17 | output fusion | flops 4915207 | bytes 9442816 | tf_op jit(solution)/shard_map/sub | solution.py:17
  394.5 6.6 %copy.21 = f32[4096,384]{1,0:T(8,128)} copy(f32[4096,384]{0,1:T(8,128)} %fusion.5) | data formatting | bytes 12582912 | tf_op jit(solution)/shard_map/sub | solution.py:17
  401.1 4.6 multiply_convert_fusion
  405.8 120.0 %all-gather.2.cloned.1.call-done = bf16[4096,1536]{1,0:T(8,128)(2,1)} async-done(((bf16[4096,384]{1,0:T(8,128)(2,1)}), bf16[4096,1536]{1,0:T(8,128)(2,1)}) %all-gather.2.cloned.1.call-update) | async-done | bytes 12582928 | tf_op jit(solution)/shard_map/all_gather | solution.py:69
  528.7 60.2 %all-reduce.2.cloned.1.call-done = bf16[512,1536]{1,0:T(8,128)(2,1)} async-done(((bf16[512,1536]{1,0:T(8,128)(2,1)}), bf16[512,1536]{1,0:T(8,128)(2,1)}) %all-reduce.2.cloned.1.call-update) | async-done | bytes 1572880 | tf_op jit(solution)/shard_map/psum | solution.py:11
  588.9 12.1 %compare_select_fusion = f32[512,4096]{1,0:T(8,128)} fusion(bf16[512,1536]{1,0:T(8,128)(2,1)} %all-reduce.2.cloned.1.call-done, bf16[4096,1536]{1,0:T(8,128)(2,1)} %all-gather.2.cloned.1.call-done, s32[4096]{0:T(1024)S(1)} %iota_add_fusion.1, s32[512]{0:T(512)S(1)} %iota_add_fusion.2), kind=kOutput, calls=%fused_computation.12 | convolution fusion | flops 6446645248 | bytes 22562816 | tf_op jit(solution)/shard_map/dot_general | solution.py:75
  (135 shorter events, 17.7 us)
Async XLA Ops:
  239.7 7.2 %copy-start = (f32[192,8]{0,1:T(8,128)S(1)}, f32[192,8]{0,1:T(8,128)}, u32[]{:S(2)}) copy-start(f32[192,8]{0,1:T(8,128)} %param.6) | copy-start | bytes 18436
  239.7 111.7 %all-to-all-start.1 = ((bf16[8,192,4,384]{3,1,2,0:T(8,128)(2,1)}), bf16[8,192,4,384]{3,1,2,0:T(8,128)(2,1)}, u32[]{:S(2)}, u32[]{:S(2)}) async-start(bf16[8,192,4,384]{3,1,2,0:T(8,128)(2,1)} %copy.17), calls=%async_computation.1 | async-start | bytes 9437184 | tf_op jit(solution)/shard_map/all_to_all | solution.py:57
  246.9 279.0 %all-gather.2.cloned.1.call-start = ((), (), s32[]{:S(2)}) async-start(), calls=%async_computation.2 | async-start | bytes 15728640 | tf_op jit(solution)/shard_map/all_gather | solution.py:69
  405.7 183.2 %all-reduce.2.cloned.1.call-start = ((), (), s32[]{:S(2)}) async-start(), calls=%async_computation.3 | async-start | bytes 3145728 | tf_op jit(solution)/shard_map/psum | solution.py:11
Sparse Core Ops, SparseCore 0:
  405.9 119.9 all-gather.1
  528.8 60.0 all-reduce.1
where the time goes:
time: 612 us; the launch traced here: 608 us
  waiting for transfers between devices  271 us (44%)
  local copies, waits for them, and re-layouts  211 us (34%)
  blocking collectives  56.3 us (9%)
  other arithmetic  35.6 us (6%)
  between operations  13.6 us (2%)
  matrix products  12.1 us (2%)
  starting transfers between devices  7.27 us (1%)
    gather x26, local copies, waits for them, and re-layouts, local(): jnp.searchsorted(row, targets, side='left')  129 us
    all_gather x1, waiting for transfers between devices, local(): full_tile = lax.all_gather(tile_block, 'gr', axis=1, tiled=True)  120 us
    all_to_all x1, waiting for transfers between devices, local(): lax.all_to_all(lax.all_to_all(outgoing, 'gr', split_axis=2, concat_axis=2...  91 us
    psum x1, waiting for transfers between devices, broadcast(): return lax.psum(jnp.where(mine, x, jnp.zeros_like(x)), axis)  60.2 us
    all_to_all x1, blocking collectives, local(): lax.all_to_all(outgoing, 'gr', split_axis=2, concat_axis=2, tiled=True)  56.3 us
    gather x2, local copies, waits for them, and re-layouts, local(): picked = jnp.take(jacobian, send_index.reshape(-1), axis=0)  23 us
    gather x2, local copies, waits for them, and re-layouts, local(): tile_block = jnp.take(incoming.reshape(-1, block_rows), flat_index, axis=0)  19.9 us
  transfers between devices with their start and end apart: 3, of which 3 were waited for; matrix products, arithmetic and copies ran while one was open for 2% of the time, Pallas kernels for 0%

commit v1 on v0

v1 whole, which is shorter than its diff:
```python
import functools

import jax
import jax.numpy as jnp
from jax import lax
from jax.experimental import pallas as pl
from jax.experimental.pallas import tpu as pltpu
from jax.sharding import PartitionSpec as P

SLAB_DEV = 512
GROUP = 256
VMEM_LIMIT = 48 * 1024 * 1024


def pick_kernel(classes, count_rows, width, index_ref, probs_ref, root_ref, jacobian_ref, *rest):
    out_refs, matrix_ref = rest[:-1], rest[-1]
    groups = matrix_ref.shape[1]

    @pl.when(pl.program_id(0) == 0)
    def _():
        down = lax.broadcasted_iota(jnp.int32, (GROUP, GROUP), 0) // classes
        across = lax.broadcasted_iota(jnp.int32, (GROUP, GROUP), 1) // classes
        for g in range(groups):
            exact = jnp.where(down == across, probs_ref[g], 0.0)
            for part in range(3):
                piece = exact.astype(jnp.bfloat16)
                matrix_ref[part, g] = piece
                exact = exact - piece.astype(jnp.float32)

    capacity = index_ref.shape[1]
    local_width = jacobian_ref.shape[0]
    lanes = lax.broadcasted_iota(jnp.int32, (capacity, local_width), 1)
    onehot = jnp.where(lanes == index_ref[0], 1.0, 0.0).astype(jnp.bfloat16)
    pieces = []
    for g in range(groups):
        span = slice(g * GROUP, (g + 1) * GROUP)
        values = jnp.dot(onehot, jacobian_ref[:, span], preferred_element_type=jnp.float32)
        short = values.astype(jnp.bfloat16)
        centre = jnp.dot(short, matrix_ref[2, g], preferred_element_type=jnp.float32)
        centre += jnp.dot(short, matrix_ref[1, g], preferred_element_type=jnp.float32)
        centre += jnp.dot(short, matrix_ref[0, g], preferred_element_type=jnp.float32)
        pieces.append((root_ref[:, span] * (values - centre)).astype(jnp.bfloat16))
    weighted = jnp.concatenate(pieces, axis=1)
    for c, out_ref in enumerate(out_refs):
        for r in range(count_rows):
            start = (r * len(out_refs) + c) * width
            out_ref[r, 0] = weighted[:, start : start + width]


def pick_rows(jacobian, probs, root, send_index, count_rows, chunks):
    count_cols, capacity = send_index.shape
    local_width, all_rows = jacobian.shape
    groups = all_rows // GROUP
    width = all_rows // count_rows // chunks
    shape = jax.ShapeDtypeStruct((count_rows, count_cols, capacity, width), jnp.bfloat16)
    return pl.pallas_call(
        functools.partial(pick_kernel, probs.shape[1], count_rows, width),
        grid=(count_cols,),
        in_specs=[
            pl.BlockSpec((1, capacity, 1), lambda t: (t, 0, 0)),
            pl.BlockSpec((groups, GROUP, 1), lambda t: (0, 0, 0)),
            pl.BlockSpec((1, all_rows), lambda t: (0, 0)),
            pl.BlockSpec((local_width, all_rows), lambda t: (0, 0)),
        ],
        out_specs=[pl.BlockSpec((count_rows, 1, capacity, width), lambda t: (0, t, 0, 0))] * chunks,
        out_shape=[shape] * chunks,
        scratch_shapes=[pltpu.VMEM((3, groups, GROUP, GROUP), jnp.bfloat16)],
        compiler_params=pltpu.CompilerParams(vmem_limit_bytes=VMEM_LIMIT),
    )(
        send_index[:, :, None],
        probs.reshape(groups, GROUP, 1),
        root.reshape(1, all_rows),
        jacobian,
    )


def product_kernel(chunks, offset_ref, *refs):
    slabs, tiles, out_ref = refs[:chunks], refs[chunks : 2 * chunks], refs[-1]
    total = None
    for slab, tile in zip(slabs, tiles):
        part = lax.dot_general(
            slab[...], tile[...], (((1,), (1,)), ((), ())), preferred_element_type=jnp.float32
        )
        total = part if total is None else total + part
    rows = offset_ref[0] + lax.broadcasted_iota(jnp.int32, out_ref.shape, 0)
    columns = (
        offset_ref[1]
        + pl.program_id(0) * out_ref.shape[1]
        + lax.broadcasted_iota(jnp.int32, out_ref.shape, 1)
    )
    out_ref[...] = jnp.where(columns <= rows, total, 0.0)


def product(slabs, tiles, offsets, tile_width):
    chunks = len(slabs)
    depth = slabs[0].shape[1]
    block = 512
    return pl.pallas_call(
        functools.partial(product_kernel, chunks),
        grid=(tile_width // block,),
        in_specs=[pl.BlockSpec(memory_space=pltpu.SMEM)]
        + [pl.BlockSpec((SLAB_DEV, depth), lambda i: (0, 0))] * chunks
        + [pl.BlockSpec((block, depth), lambda i: (i, 0))] * chunks,
        out_specs=pl.BlockSpec((SLAB_DEV, block), lambda i: (0, i)),
        out_shape=jax.ShapeDtypeStruct((SLAB_DEV, tile_width), jnp.float32),
        compiler_params=pltpu.CompilerParams(vmem_limit_bytes=VMEM_LIMIT),
    )(offsets, *slabs, *tiles)


def local(jacobian, class_scores, source):
    count_rows = lax.axis_size("gr")
    count_cols = lax.axis_size("gc")
    grid_row = lax.axis_index("gr")
    grid_col = lax.axis_index("gc")
    myself = grid_row * count_cols + grid_col
    local_width, all_rows = jacobian.shape
    total_weights = source.shape[0]
    tile_width = total_weights // count_cols
    capacity = 3 * (total_weights // (count_cols * count_cols * count_rows)) // 2
    block_rows = all_rows // count_rows
    chunks = block_rows // 128 if block_rows % 128 == 0 else 1
    width = block_rows // chunks
    slab_total = SLAB_DEV * count_rows
    probs = class_scores / jnp.sum(class_scores, axis=1, keepdims=True)
    root = jnp.sqrt(probs)

    tiles = source.reshape(count_cols, tile_width)
    owned = tiles // local_width == myself
    rank = jnp.where(owned, jnp.cumsum(owned.astype(jnp.int32), axis=1) - 1, -1)
    slots = jnp.arange(capacity, dtype=jnp.int32)
    hit = rank[:, None, :] == slots[None, :, None]
    send_index = jnp.sum(jnp.where(hit, (tiles % local_width + 1)[:, None, :], 0), axis=2) - 1
    outgoing = pick_rows(jacobian, probs, root, send_index, count_rows, chunks)

    tile_source = (
        lax.dynamic_slice_in_dim(source, grid_col * tile_width, tile_width, 0) // local_width
    )
    onehot = (
        tile_source[:, None] == jnp.arange(count_rows * count_cols, dtype=jnp.int32)[None, :]
    ).astype(jnp.int32)
    arrival = jnp.sum(jnp.cumsum(onehot, axis=0) * onehot, axis=1) - 1
    flat_index = tile_source * capacity + arrival

    slab_list, tile_list = [], []
    for part in outgoing:
        incoming = lax.all_to_all(
            part.reshape(-1, capacity, width), ("gr", "gc"), split_axis=0, concat_axis=0, tiled=True
        )
        block = incoming.reshape(-1, width).at[flat_index].get(mode="promise_in_bounds")
        full = lax.all_gather(block, "gr", axis=1, tiled=True)
        piece = lax.dynamic_slice_in_dim(
            full, tile_width - slab_total + grid_row * SLAB_DEV, SLAB_DEV, 0
        )
        mine = grid_col == count_cols - 1
        slab_list.append(lax.psum(jnp.where(mine, piece, jnp.zeros_like(piece)), "gc"))
        tile_list.append(full)
    offsets = jnp.stack(
        [total_weights - slab_total + grid_row * SLAB_DEV, grid_col * tile_width]
    ).astype(jnp.int32)
    return product(slab_list, tile_list, offsets, tile_width)


def solution(mesh):
    in_specs = (P(("gr", "gc"), None), P(), P())
    out_specs = P("gr", "gc")
    return jax.shard_map(local, mesh=mesh, in_specs=in_specs, out_specs=out_specs, check_vma=False)
```

time: 612 us -> 386 us (0.63)
  local copies, waits for them, and re-layouts: 211 us -> 58.5 us
  waiting for transfers between devices: 271 us -> 135 us
  Pallas kernels: 0 us -> 48.3 us
  blocking collectives: 56.3 us -> 82.4 us
  matrix products: 12.1 us -> 0 us
    gather x33 -> x3, local copies, waits for them, and re-layouts: 182 us -> 46.9 us  [local(): incoming.reshape(-1, width).at[flat_index].get(mode='promise_in_bounds')]
    all_to_all x1, waiting for transfers between devices: 91 us -> 13.5 us  [local(): lax.all_to_all(part.reshape(-1, capacity, width), ('gr', 'gc'), split_axi...]
    all_gather x1 -> x3, waiting for transfers between devices: 120 us -> 59.8 us  [local(): full = lax.all_gather(block, 'gr', axis=1, tiled=True)]
    pallas_call x0 -> x2, Pallas kernels: none -> 48.3 us  [the longest x1 36 us: pick_rows(): pl.pallas_call(functools.partial(pick_kernel, probs.shape[1], count_rows,...]
    all_to_all x1 -> x2, blocking collectives: 56.3 us -> 82.4 us  [local(): lax.all_to_all(part.reshape(-1, capacity, width), ('gr', 'gc'), split_axi...]
    dot_general x1 -> x0, matrix products: 12.1 us -> none  [local(): lax.dot_general(slab_part, full_tile, (((1,), (1,)), ((), ())), preferred...]
    all_to_all x2 -> x0, local copies, waits for them, and re-layouts: 10.9 us -> none  [the longest x1 8.17 us: local(): lax.all_to_all(lax.all_to_all(outgoing, 'gr', split_axis=2, concat_axis=2...]
    another operation x5 -> x6, other arithmetic: 12.1 us -> 22 us
  transfers between devices with their start and end apart: 3 -> 5, of which waited for: 3 -> 4; matrix products, arithmetic and copies ran while one was open for 2% -> 16% of each run, Pallas kernels for 0% -> 0%
where the time goes in v1:
time: 386 us; the launch traced here: 382 us
  waiting for transfers between devices  135 us (35%)
  blocking collectives  82.4 us (21%)
  local copies, waits for them, and re-layouts  58.5 us (15%)
  Pallas kernels  48.3 us (13%)
  other arithmetic  37.4 us (10%)
  between operations  13.3 us (3%)
  starting transfers between devices  7.26 us (2%)
    all_to_all x2, blocking collectives, local(): lax.all_to_all(part.reshape(-1, capacity, width), ('gr', 'gc'), split_axi...  82.4 us
    psum x1, waiting for transfers between devices, local(): lax.psum(jnp.where(mine, piece, jnp.zeros_like(piece)), 'gc')  61.2 us
    all_gather x3, waiting for transfers between devices, local(): full = lax.all_gather(block, 'gr', axis=1, tiled=True)  59.8 us
    gather x3, local copies, waits for them, and re-layouts, local(): incoming.reshape(-1, width).at[flat_index].get(mode='promise_in_bounds')  46.9 us
    pallas_call x1, Pallas kernels, pick_rows(): pl.pallas_call(functools.partial(pick_kernel, probs.shape[1], count_rows,...  36 us
    another operation x5, other arithmetic  21.9 us
    all_to_all x1, waiting for transfers between devices, local(): lax.all_to_all(part.reshape(-1, capacity, width), ('gr', 'gc'), split_axi...  13.5 us
    pallas_call x1, Pallas kernels, product(): pl.pallas_call(functools.partial(product_kernel, chunks), grid=(tile_widt...  12.3 us
  transfers between devices with their start and end apart: 5, of which 4 were waited for; matrix products, arithmetic and copies ran while one was open for 16% of the time, Pallas kernels for 0%

profile of v1, /device:TPU:1, one launch (start us, length us, event | category | flops | bytes accessed | tf_op | source)
XLA Modules:
  0.0 381.6 jit_solution(16401142423089329893)
XLA Ops:
  8.3 0.9 reshape.136
  9.3 1.0 fusion.9
  10.3 2.3 reduce-window.14
  13.3 3.5 select_reduce_fusion
  17.4 36.0 %shard_map.37 = (bf16[4,8,192,128]{3,2,1,0:T(8,128)(2,1)S(1)}, bf16[4,8,192,128]{3,2,1,0:T(8,128)(2,1)S(1)}, bf16[4,8,192,128]{3,2,1,0:T(8,128)(2,1)}) custom-call(s32[8,192,1]{2,1,0:T(8,128)S(1)} %copy.12.index_ref, f32[6,256,1]{2,1,0:T(8,128)S(1)} %reshape.178.probs_ref, f32[1,1536]{1,0:T(1,128)S(1)} %reshape.140.root_ref, bf16[2048,1536]{1,0:T(8,128)(2,1)} %jacobian_ref.1), custom_call_target="tpu_custom_call" | custom-call | tf_op jit(solution)/shard_map/pallas_call | solution.py:56
  53.4 1.2 copy-done.1
  54.6 7.1 %all-to-all-start.2 = ((bf16[32,192,128]{2,1,0:T(8,128)(2,1)}), bf16[32,192,128]{2,1,0:T(8,128)(2,1)S(1)}, u32[]{:S(2)}, u32[]{:S(2)}) async-start(bf16[32,192,128]{2,1,0:T(8,128)(2,1)} %bitcast.38), calls=%async_computation.2 | async-start | bytes 3145728 | tf_op jit(solution)/shard_map/all_to_all | solution.py:146
  61.8 0.7 fusion.15
  62.5 0.9 fusion.2
  63.4 18.0 %reduce-window.16 = s32[32,32,128]{2,1,0:T(8,128)} reduce-window(s32[32,32,128]{2,1,0:T(8,128)} %fusion.2, s32[]{:T(128)} %constant.71.clone.1), window={size=1x1x128 pad=0_0x0_0x127_0}, to_apply=%region_4.5 | reduce-window | flops 16646144 | bytes 1048580 | tf_op jit(solution)/shard_map/reduce-window.2
  81.4 1.8 slice_reduce_fusion
  83.4 0.7 add_select_fusion.3
  84.1 1.2 broadcast_add_fusion
  85.7 0.7 fusion.12
  86.5 13.5 %all-to-all-done.2 = bf16[32,192,128]{2,1,0:T(8,128)(2,1)S(1)} async-done(((bf16[32,192,128]{2,1,0:T(8,128)(2,1)}), bf16[32,192,128]{2,1,0:T(8,128)(2,1)S(1)}, u32[]{:S(2)}, u32[]{:S(2)}) %all-to-all-start.2) | async-done | bytes 1572896 | tf_op jit(solution)/shard_map/all_to_all | solution.py:146
  100.0 1.1 copy-done.6
  101.1 16.0 %gather_fusion.2 = bf16[4096,128]{1,0:T(8,128)(2,1)} fusion(bf16[6144,128]{1,0:T(8,128)(2,1)} %bitcast.34, s32[4096]{0:T(1024)S(1)} %fusion.12), kind=kCustom, calls=%fused_computation.2 | custom fusion | bytes 2113536 | tf_op jit(solution)/shard_map/gather | solution.py:149
  117.2 41.6 %all_to_all.15 = bf16[32,192,128]{2,1,0:T(8,128)(2,1)} all-to-all(bf16[32,192,128]{2,1,0:T(8,128)(2,1)S(1)} %bitcast.33), channel_id=1, replica_groups=mesh['gr'=4,'gc'=8] {'gr','gc'}, dimensions={0} | all-to-all | bytes 3145728 | tf_op jit(solution)/shard_map/all_to_all | solution.py:146
  158.8 16.0 %gather_fusion = bf16[4096,128]{1,0:T(8,128)(2,1)} fusion(bf16[6144,128]{1,0:T(8,128)(2,1)} %bitcast.36, s32[4096]{0:T(1024)S(1)} %fusion.12), kind=kCustom, calls=%fused_computation | custom fusion | bytes 2113536 | tf_op jit(solution)/shard_map/gather | solution.py:149
  174.9 40.7 %all_to_all.16 = bf16[32,192,128]{2,1,0:T(8,128)(2,1)S(1)} all-to-all(bf16[32,192,128]{2,1,0:T(8,128)(2,1)S(1)} %bitcast.32), channel_id=1, replica_groups=mesh['gr'=4,'gc'=8] {'gr','gc'}, dimensions={0} | all-to-all | bytes 3145728 | tf_op jit(solution)/shard_map/all_to_all | solution.py:146
  215.7 14.9 %gather_fusion.1 = bf16[4096,128]{1,0:T(8,128)(2,1)} fusion(bf16[6144,128]{1,0:T(8,128)(2,1)S(1)} %bitcast.35, s32[4096]{0:T(1024)S(1)} %fusion.12), kind=kCustom, calls=%fused_computation.1 | custom fusion | bytes 2113536 | tf_op jit(solution)/shard_map/gather | solution.py:149
  230.7 1.9 dynamic-slice_select_fusion
  232.6 7.2 %all-gather.7.cloned.1.call-done.refs_3_ = bf16[4096,512]{1,0:T(8,128)(2,1)} async-done(((bf16[4096,128]{1,0:T(8,128)(2,1)}), bf16[4096,512]{1,0:T(8,128)(2,1)}) %all-gather.7.cloned.1.call-update) | async-done | bytes 4194320 | tf_op jit(solution)/shard_map/all_gather | solution.py:150
  239.8 1.9 dynamic-slice_select_fusion.2
  241.8 52.5 %all-gather.9.cloned.1.call-done.refs_4_ = bf16[4096,512]{1,0:T(8,128)(2,1)} async-done(((bf16[4096,128]{1,0:T(8,128)(2,1)}), bf16[4096,512]{1,0:T(8,128)(2,1)}) %all-gather.9.cloned.1.call-update) | async-done | bytes 4194320 | tf_op jit(solution)/shard_map/all_gather | solution.py:150
  294.3 1.9 dynamic-slice_select_fusion.1
  296.3 61.2 %all-reduce.3.cloned.1.call-done = (bf16[512,512]{1,0:T(8,128)(2,1)}, bf16[512,512]{1,0:T(8,128)(2,1)}, bf16[512,512]{1,0:T(8,128)(2,1)}) async-done(((bf16[512,512]{1,0:T(8,128)(2,1)}, bf16[512,512]{1,0:T(8,128)(2,1)}, bf16[512,512]{1,0:T(8,128)(2,1)}), (bf16[512,512]{1,0:T(8,128)(2,1)}, bf16[512,512]{1,0:T(8,128)(2,1)}, bf16[512,512]{1,0:T(8,128)(2,1)})) %all-reduce.3.cloned.1.call-update) | async-done | bytes 1572880 | tf_op jit(solution)/shard_map/psum | solution.py:155
  357.5 2.2 copy-done
  359.7 1.0 copy-done.3
  360.7 1.0 copy-done.4
  361.8 1.0 copy-done.5
  362.8 12.3 %shard_map.38 = f32[512,4096]{1,0:T(8,128)} custom-call(s32[2]{0:T(128)S(1)} %pad_add_fusion.offset_ref, bf16[512,512]{1,0:T(8,128)(2,1)S(1)} %copy-done.3, bf16[512,512]{1,0:T(8,128)(2,1)S(1)} %copy-done.4, bf16[512,512]{1,0:T(8,128)(2,1)S(1)} %copy-done.5, bf16[4096,512]{1,0:T(8,128)(2,1)S(1)} %copy-done, ...), custom_call_target="tpu_custom_call" | custom-call | tf_op jit(solution)/shard_map/pallas_call | solution.py:98
  (32 shorter events, 3.9 us)
Async XLA Ops:
  53.4 1.2 copy-start.1
  54.6 45.4 %all-to-all-start.2 = ((bf16[32,192,128]{2,1,0:T(8,128)(2,1)}), bf16[32,192,128]{2,1,0:T(8,128)(2,1)S(1)}, u32[]{:S(2)}, u32[]{:S(2)}) async-start(bf16[32,192,128]{2,1,0:T(8,128)(2,1)} %bitcast.38), calls=%async_computation.2 | async-start | bytes 3145728 | tf_op jit(solution)/shard_map/all_to_all | solution.py:146
  61.7 168.9 %all-gather.11.cloned.1.call-start = ((), (), s32[]{:S(2)}) async-start(), calls=%async_computation.5 | async-start | bytes 5242880 | tf_op jit(solution)/shard_map/all_gather | solution.py:150
  100.0 1.1 copy-start.6
  101.1 16.0 %copy-start.2 = (bf16[4,8,192,128]{3,2,1,0:T(8,128)(2,1)S(1)}, bf16[4,8,192,128]{3,2,1,0:T(8,128)(2,1)}, u32[]{:S(2)}) copy-start(bf16[4,8,192,128]{3,2,1,0:T(8,128)(2,1)} %copy-done.1) | copy-start | bytes 4718596
  117.1 122.7 %all-gather.7.cloned.1.call-start = ((), (), s32[]{:S(2)}) async-start(), calls=%async_computation.3 | async-start | bytes 5242880 | tf_op jit(solution)/shard_map/all_gather | solution.py:150
  174.9 119.4 %all-gather.9.cloned.1.call-start = ((), (), s32[]{:S(2)}) async-start(), calls=%async_computation.4 | async-start | bytes 5242880 | tf_op jit(solution)/shard_map/all_gather | solution.py:150
  230.6 126.9 %all-reduce.3.cloned.1.call-start = ((), (), s32[]{:S(2)}) async-start(), calls=%async_computation.6 | async-start | bytes 3145728 | tf_op jit(solution)/shard_map/psum | solution.py:155
  357.5 2.2 copy-start
  359.7 1.0 copy-start.3
  360.7 1.0 copy-start.4
  361.8 1.0 copy-start.5
Sparse Core Ops, SparseCore 0:
  117.2 62.6 all-gather.10
  181.7 58.0 all-gather.6
  241.7 52.5 all-gather.8
  296.7 60.7 all-reduce.2

commit v2 on v1

v2 whole, which is shorter than its diff:
```python
import functools

import jax
import jax.numpy as jnp
from jax import lax
from jax.experimental import pallas as pl
from jax.experimental.pallas import tpu as pltpu
from jax.sharding import PartitionSpec as P

SLAB_DEV = 512
GROUP = 256
PICK_ROWS = 768
VMEM_LIMIT = 48 * 1024 * 1024


def pick_kernel(classes, count_rows, index_ref, probs_ref, root_ref, jacobian_ref, *rest):
    out_refs, matrix_ref = rest[:-1], rest[-1]
    groups = matrix_ref.shape[1]

    @pl.when(pl.program_id(0) == 0)
    def _():
        down = lax.broadcasted_iota(jnp.int32, (GROUP, GROUP), 0) // classes
        across = lax.broadcasted_iota(jnp.int32, (GROUP, GROUP), 1) // classes
        for g in range(groups):
            exact = jnp.where(down == across, probs_ref[g], 0.0)
            for part in range(3):
                piece = exact.astype(jnp.bfloat16)
                matrix_ref[part, g] = piece
                exact = exact - piece.astype(jnp.float32)

    steps, capacity = out_refs[0].shape[1:3]
    local_width, all_rows = jacobian_ref.shape
    lanes = lax.broadcasted_iota(jnp.int32, (steps * capacity, local_width), 1)
    onehot = jnp.where(lanes == index_ref[...], 1.0, 0.0).astype(jnp.bfloat16)
    pieces = []
    for g in range(groups):
        span = slice(g * GROUP, (g + 1) * GROUP)
        values = jnp.dot(onehot, jacobian_ref[:, span], preferred_element_type=jnp.float32)
        short = values.astype(jnp.bfloat16)
        centre = jnp.dot(short, matrix_ref[2, g], preferred_element_type=jnp.float32)
        centre += jnp.dot(short, matrix_ref[1, g], preferred_element_type=jnp.float32)
        centre += jnp.dot(short, matrix_ref[0, g], preferred_element_type=jnp.float32)
        pieces.append((root_ref[:, span] * (values - centre)).astype(jnp.bfloat16))
    weighted = jnp.concatenate(pieces, axis=1)
    for r in range(count_rows):
        start = r * (all_rows // count_rows)
        for out_ref in out_refs:
            width = out_ref.shape[3]
            for t in range(steps):
                rows = slice(t * capacity, (t + 1) * capacity)
                out_ref[r, t] = weighted[rows, start : start + width]
            start += width


def pick_rows(jacobian, probs, root, send_index, count_rows, widths):
    count_cols, capacity = send_index.shape
    local_width, all_rows = jacobian.shape
    groups = all_rows // GROUP
    steps = max(1, min(count_cols, PICK_ROWS // capacity))
    shapes = [(count_rows, count_cols, capacity, width) for width in widths]
    return pl.pallas_call(
        functools.partial(pick_kernel, probs.shape[1], count_rows),
        grid=(count_cols // steps,),
        in_specs=[
            pl.BlockSpec((steps * capacity, 1), lambda t: (t, 0)),
            pl.BlockSpec((groups, GROUP, 1), lambda t: (0, 0, 0)),
            pl.BlockSpec((1, all_rows), lambda t: (0, 0)),
            pl.BlockSpec((local_width, all_rows), lambda t: (0, 0)),
        ],
        out_specs=[
            pl.BlockSpec((count_rows, steps, capacity, width), lambda t: (0, t, 0, 0))
            for width in widths
        ],
        out_shape=[jax.ShapeDtypeStruct(shape, jnp.bfloat16) for shape in shapes],
        scratch_shapes=[pltpu.VMEM((3, groups, GROUP, GROUP), jnp.bfloat16)],
        compiler_params=pltpu.CompilerParams(vmem_limit_bytes=VMEM_LIMIT),
    )(
        send_index.reshape(-1, 1),
        probs.reshape(groups, GROUP, 1),
        root.reshape(1, all_rows),
        jacobian,
    )


def product_kernel(chunks, offset_ref, *refs):
    slabs, tiles, out_ref = refs[:chunks], refs[chunks:-1], refs[-1]
    count = slabs[0].shape[0]
    total = None
    for c, slab in enumerate(slabs):
        for d in range(count):
            part = lax.dot_general(
                slab[d],
                tiles[c * count + d][...],
                (((1,), (1,)), ((), ())),
                preferred_element_type=jnp.float32,
            )
            total = part if total is None else total + part
    rows = offset_ref[0] + lax.broadcasted_iota(jnp.int32, out_ref.shape, 0)
    columns = (
        offset_ref[1]
        + pl.program_id(0) * out_ref.shape[1]
        + lax.broadcasted_iota(jnp.int32, out_ref.shape, 1)
    )
    out_ref[...] = jnp.where(columns <= rows, total, 0.0)


def product(slabs, tiles, offsets, tile_width):
    block = 512
    return pl.pallas_call(
        functools.partial(product_kernel, len(slabs)),
        grid=(tile_width // block,),
        in_specs=[pl.BlockSpec(memory_space=pltpu.SMEM)]
        + [pl.BlockSpec(slab.shape, lambda i: (0, 0, 0)) for slab in slabs]
        + [pl.BlockSpec((block, tile.shape[1]), lambda i: (i, 0)) for tile in tiles],
        out_specs=pl.BlockSpec((SLAB_DEV, block), lambda i: (0, i)),
        out_shape=jax.ShapeDtypeStruct((SLAB_DEV, tile_width), jnp.float32),
        compiler_params=pltpu.CompilerParams(vmem_limit_bytes=VMEM_LIMIT),
    )(offsets, *slabs, *tiles)


def exchange(x, count, d):
    return lax.ppermute(x, "gr", [(i, i ^ d) for i in range(count)])


def gather_pieces(block, count):
    if count != 4:
        return [block] + [exchange(block, count, d) for d in range(1, count)]
    half = block.shape[0] // 2
    one, two = exchange(block, 4, 1), exchange(block, 4, 2)
    top, bottom = exchange(one[:half], 4, 2), exchange(two[half:], 4, 1)
    return [block, one, two, jnp.concatenate([top, bottom])]


def spread_slab(block, count_rows, count_cols, grid_row, grid_col):
    first = block.shape[0] - SLAB_DEV * count_rows
    last = count_cols - 1

    def rows_of(r):
        return lax.dynamic_slice_in_dim(block, first + r * SLAB_DEV, SLAB_DEV, 0)

    own = rows_of(grid_row)
    parts = [jnp.where(grid_col == last, own, jnp.zeros_like(own))]
    for d in range(1, count_rows):
        pairs = [
            (r * count_cols + last, (r ^ d) * count_cols + last) for r in range(count_rows)
        ]
        parts.append(lax.ppermute(rows_of(grid_row ^ d), ("gr", "gc"), pairs))
    slab = jnp.stack(parts)
    stride = count_cols // 2
    while stride:
        pairs = [(c, c - stride) for c in range(last, 0, -2 * stride)]
        slab = slab + lax.ppermute(slab, "gc", pairs)
        stride //= 2
    return slab


def local(jacobian, class_scores, source):
    count_rows = lax.axis_size("gr")
    count_cols = lax.axis_size("gc")
    grid_row = lax.axis_index("gr")
    grid_col = lax.axis_index("gc")
    myself = grid_row * count_cols + grid_col
    local_width, all_rows = jacobian.shape
    total_weights = source.shape[0]
    tile_width = total_weights // count_cols
    capacity = 3 * (total_weights // (count_cols * count_cols * count_rows)) // 2
    block_rows = all_rows // count_rows
    widths = [block_rows]
    if block_rows % 384 == 0:
        widths = [2 * block_rows // 3, block_rows // 3]
    slab_total = SLAB_DEV * count_rows
    probs = class_scores / jnp.sum(class_scores, axis=1, keepdims=True)
    root = jnp.sqrt(probs)

    tiles = source.reshape(count_cols, tile_width)
    owned = tiles // local_width == myself
    rank = jnp.where(owned, jnp.cumsum(owned.astype(jnp.int32), axis=1) - 1, -1)
    slots = jnp.arange(capacity, dtype=jnp.int32)
    hit = rank[:, None, :] == slots[None, :, None]
    send_index = jnp.sum(jnp.where(hit, (tiles % local_width + 1)[:, None, :], 0), axis=2) - 1
    outgoing = pick_rows(jacobian, probs, root, send_index, count_rows, widths)

    tile_source = (
        lax.dynamic_slice_in_dim(source, grid_col * tile_width, tile_width, 0) // local_width
    )
    onehot = (
        tile_source[:, None] == jnp.arange(count_rows * count_cols, dtype=jnp.int32)[None, :]
    ).astype(jnp.int32)
    arrival = jnp.sum(jnp.cumsum(onehot, axis=0) * onehot, axis=1) - 1
    flat_index = tile_source * capacity + arrival

    slab_list, tile_list = [], []
    for part, width in zip(outgoing, widths):
        incoming = lax.all_to_all(
            part.reshape(-1, capacity, width), ("gr", "gc"), split_axis=0, concat_axis=0, tiled=True
        )
        block = incoming.reshape(-1, width).at[flat_index].get(mode="promise_in_bounds")
        tile_list += gather_pieces(block, count_rows)
        slab_list.append(spread_slab(block, count_rows, count_cols, grid_row, grid_col))
    offsets = jnp.stack(
        [total_weights - slab_total + grid_row * SLAB_DEV, grid_col * tile_width]
    ).astype(jnp.int32)
    return product(slab_list, tile_list, offsets, tile_width)


def solution(mesh):
    in_specs = (P(("gr", "gc"), None), P(), P())
    out_specs = P("gr", "gc")
    return jax.shard_map(local, mesh=mesh, in_specs=in_specs, out_specs=out_specs, check_vma=False)
```

time: 386 us -> 326 us (0.84)
  waiting for transfers between devices: 135 us -> 97.2 us
  local copies, waits for them, and re-layouts: 58.5 us -> 37.2 us
  starting transfers between devices: 7.26 us -> 22.7 us
  between operations: 13.3 us -> 0.58 us
  other arithmetic: 37.4 us -> 41.5 us
    ppermute x0 -> x20, waiting for transfers between devices: none -> 97.2 us  [the longest x8 52.9 us: exchange(): return lax.ppermute(x, 'gr', [(i, i ^ d) for i in range(count)])]
    psum x1 -> x0, waiting for transfers between devices: 61.2 us -> none  [local(): lax.psum(jnp.where(mine, piece, jnp.zeros_like(piece)), 'gc')]
    all_gather x3 -> x0, waiting for transfers between devices: 59.8 us -> none  [local(): full = lax.all_gather(block, 'gr', axis=1, tiled=True)]
    ppermute x0 -> x20, starting transfers between devices: none -> 18.9 us  [the longest x6 7.8 us: spread_slab(): slab = slab + lax.ppermute(slab, 'gc', pairs)]
    gather x3 -> x2, local copies, waits for them, and re-layouts: 46.9 us -> 29.6 us  [local(): incoming.reshape(-1, width).at[flat_index].get(mode='promise_in_bounds')]
    all_to_all x1, waiting for transfers between devices: 13.5 us -> 0.01 us  [local(): lax.all_to_all(part.reshape(-1, capacity, width), ('gr', 'gc'), split_axi...]
    unnamed x14 -> x34, local copies, waits for them, and re-layouts: 7.63 us -> 0.73 us
    add x0 -> x6, other arithmetic: none -> 6.69 us  [spread_slab(): slab = slab + lax.ppermute(slab, 'gc', pairs)]
  transfers between devices with their start and end apart: 5 -> 21, of which waited for: 4 -> 3; matrix products, arithmetic and copies ran while one was open for 16% -> 21% of each run, Pallas kernels for 0% -> 0%
where the time goes in v2:
time: 326 us; the launch traced here: 323 us
  waiting for transfers between devices  97.2 us (30%)
  blocking collectives  79 us (24%)
  Pallas kernels  44.6 us (14%)
  other arithmetic  41.5 us (13%)
  local copies, waits for them, and re-layouts  37.2 us (11%)
  starting transfers between devices  22.7 us (7%)
    all_to_all x1, blocking collectives, local(): lax.all_to_all(part.reshape(-1, capacity, width), ('gr', 'gc'), split_axi...  79 us
    ppermute x8, waiting for transfers between devices, exchange(): return lax.ppermute(x, 'gr', [(i, i ^ d) for i in range(count)])  52.9 us
    ppermute x6, waiting for transfers between devices, spread_slab(): slab = slab + lax.ppermute(slab, 'gc', pairs)  44.2 us
    pallas_call x1, Pallas kernels, pick_rows(): pl.pallas_call(functools.partial(pick_kernel, probs.shape[1], count_rows)...  31.1 us
    gather x2, local copies, waits for them, and re-layouts, local(): incoming.reshape(-1, width).at[flat_index].get(mode='promise_in_bounds')  29.6 us
    another operation x5, other arithmetic  21.9 us
    pallas_call x1, Pallas kernels, product(): pl.pallas_call(functools.partial(product_kernel, len(slabs)), grid=(tile_...  13.5 us
    ppermute x6, starting transfers between devices, spread_slab(): slab = slab + lax.ppermute(slab, 'gc', pairs)  7.8 us
  transfers between devices with their start and end apart: 21, of which 3 were waited for; matrix products, arithmetic and copies ran while one was open for 21% of the time, Pallas kernels for 0%

profile of v2, /device:TPU:1, one launch (start us, length us, event | category | flops | bytes accessed | tf_op | source)
XLA Modules:
  0.0 322.8 jit_solution(16072574069293314050)
XLA Ops:
  1.8 0.9 reshape.134
  2.7 1.0 fusion.9
  3.7 2.3 reduce-window.14
  6.8 3.6 %select_reduce_fusion = s32[8,192]{1,0:T(8,128)S(1)} fusion(s32[8,4096]{1,0:T(8,128)S(1)} %get-tuple-element.20, s32[8,4096]{1,0:T(8,128)S(1)} %get-tuple-element.19), kind=kLoop, calls=%fused_computation.2 | loop fusion | flops 18872832 | bytes 268288 | tf_op jit(solution)/shard_map/reduce_sum | solution.py:180
  11.3 31.1 %shard_map.37 = (bf16[4,8,192,256]{3,2,1,0:T(8,128)(2,1)}, bf16[4,8,192,128]{3,2,1,0:T(8,128)(2,1)}) custom-call(s32[1536,1]{1,0:T(8,128)S(1)} %sub.37.index_ref, f32[6,256,1]{2,1,0:T(8,128)S(1)} %reshape.162.probs_ref, f32[1,1536]{1,0:T(1,128)S(1)} %reshape.138.root_ref, bf16[2048,1536]{1,0:T(8,128)(2,1)} %jacobian_ref.1), custom_call_target="tpu_custom_call" | custom-call | tf_op jit(solution)/shard_map/pallas_call | solution.py:61
  42.3 79.0 %all_to_all.10 = bf16[32,192,256]{2,1,0:T(8,128)(2,1)S(1)} all-to-all(bf16[32,192,256]{2,1,0:T(8,128)(2,1)} %bitcast.39), channel_id=1, replica_groups=mesh['gr'=4,'gc'=8] {'gr','gc'}, dimensions={0} | all-to-all | bytes 6291456 | tf_op jit(solution)/shard_map/all_to_all | solution.py:194
  121.4 3.8 %all-to-all-start.1 = ((bf16[32,192,128]{2,1,0:T(8,128)(2,1)}), bf16[32,192,128]{2,1,0:T(8,128)(2,1)}, u32[]{:S(2)}, u32[]{:S(2)}) async-start(bf16[32,192,128]{2,1,0:T(8,128)(2,1)} %bitcast.11), calls=%async_computation.1 | async-start | bytes 3145728 | tf_op jit(solution)/shard_map/all_to_all | solution.py:194
  126.8 18.0 %reduce-window.16 = s32[32,32,128]{2,1,0:T(8,128)} reduce-window(s32[32,32,128]{2,1,0:T(8,128)} %fusion.2, s32[]{:T(128)} %constant.78.clone.1), window={size=1x1x128 pad=0_0x0_0x127_0}, to_apply=%region_4.5 | reduce-window | flops 16646144 | bytes 1048580 | tf_op jit(solution)/shard_map/reduce-window.2
  144.8 1.8 slice_reduce_fusion
  147.6 1.2 broadcast_add_fusion
  149.9 17.0 %gather_fusion = bf16[4096,256]{1,0:T(8,128)(2,1)} fusion(bf16[6144,256]{1,0:T(8,128)(2,1)S(1)} %bitcast.38, s32[4096]{0:T(1024)S(1)} %fusion.12), kind=kCustom, calls=%fused_computation | custom fusion | bytes 4210688 | tf_op jit(solution)/shard_map/gather | solution.py:197
  166.9 1.3 select_bitcast_fusion
  171.1 1.6 collective-permute-start.3
  172.7 1.4 collective-permute-start.12
  174.1 1.2 collective-permute-start.13
  175.3 12.6 %gather_fusion.1 = bf16[4096,128]{1,0:T(8,128)(2,1)S(1)} fusion(bf16[6144,128]{1,0:T(8,128)(2,1)} %bitcast.12, s32[4096]{0:T(1024)S(1)} %fusion.12), kind=kCustom, calls=%fused_computation.1 | custom fusion | bytes 2113536 | tf_op jit(solution)/shard_map/gather | solution.py:197
  191.5 2.4 fusion.15
  193.9 1.3 collective-permute-start.4
  196.2 46.0 %collective-permute-done.16.refs_7_ = bf16[4096,128]{1,0:T(8,128)(2,1)S(1)} collective-permute-done((bf16[4096,128]{1,0:T(8,128)(2,1)S(1)}, bf16[4096,128]{1,0:T(8,128)(2,1)S(1)}, u32[]{:S(2)}, u32[]{:S(2)}) %collective-permute-start.16) | collective-permute-done | bytes 1048608 | tf_op jit(solution)/shard_map/ppermute | solution.py:122
  242.1 1.5 collective-permute-start.10
  243.7 1.6 collective-permute-start.18
  245.4 1.3 collective-permute-start.19
  246.7 1.3 slice.39
  248.3 1.3 slice.40
  249.6 44.2 %collective-permute-done.10 = bf16[4,512,128]{2,1,0:T(8,128)(2,1)} collective-permute-done((bf16[4,512,128]{2,1,0:T(8,128)(2,1)}, bf16[4,512,128]{2,1,0:T(8,128)(2,1)}, u32[]{:S(2)}, u32[]{:S(2)}) %collective-permute-start.10) | collective-permute-done | bytes 524320 | tf_op jit(solution)/shard_map/ppermute | solution.py:152
  294.5 1.1 fusion.17
  295.7 1.3 collective-permute-start.11
  297.0 1.8 fusion.18
  298.8 1.4 collective-permute-start.5
  300.5 7.0 %collective-permute-done.15 = bf16[2048,256]{1,0:T(8,128)(2,1)S(1)} collective-permute-done((bf16[2048,256]{1,0:T(8,128)(2,1)S(1)}, bf16[2048,256]{1,0:T(8,128)(2,1)S(1)}, u32[]{:S(2)}, u32[]{:S(2)}) %collective-permute-start.15) | collective-permute-done | bytes 1048608 | tf_op jit(solution)/shard_map/ppermute | solution.py:122
  307.5 1.5 pad_maximum_fusion.refs_5_
  309.3 13.5 %shard_map.38 = f32[512,4096]{1,0:T(8,128)} custom-call(s32[2]{0:T(128)S(1)} %pad_add_fusion.offset_ref, bf16[4,512,256]{2,1,0:T(8,128)(2,1)S(1)} %add.127.refs_0_, bf16[4,512,128]{2,1,0:T(8,128)(2,1)S(1)} %add.130.refs_1_, bf16[4096,256]{1,0:T(8,128)(2,1)} %gather_fusion, bf16[4096,256]{1,0:T(8,128)(2,1)} %collective-permute-done.12.refs_3_, ...), custom_call_target="tpu_custom_call" | custom-call | tf_op jit(solution)/shard_map/pallas_call | solution.py:109
  (91 shorter events, 15.9 us)
Async XLA Ops:
  121.4 54.0 %all-to-all-start.1 = ((bf16[32,192,128]{2,1,0:T(8,128)(2,1)}), bf16[32,192,128]{2,1,0:T(8,128)(2,1)}, u32[]{:S(2)}, u32[]{:S(2)}) async-start(bf16[32,192,128]{2,1,0:T(8,128)(2,1)} %bitcast.11), calls=%async_computation.1 | async-start | bytes 3145728 | tf_op jit(solution)/shard_map/all_to_all | solution.py:194
  168.1 2.1 collective-permute-start.2
  168.8 1.4 collective-permute-start.1
  169.5 0.7 collective-permute-start
  171.1 20.3 %collective-permute-start.3 = (bf16[4,512,256]{2,1,0:T(8,128)(2,1)S(1)}, bf16[4,512,256]{2,1,0:T(8,128)(2,1)}, u32[]{:S(2)}, u32[]{:S(2)}) collective-permute-start(bf16[4,512,256]{2,1,0:T(8,128)(2,1)S(1)} %pad_maximum_fusion.1), channel_id=1, source_target_pairs={{7,3},{15,11},{23,19},{31,27}} | collective-permute-start | bytes 3145736 | tf_op jit(solution)/shard_map/ppermute | solution.py:152
  172.7 72.7 %collective-permute-start.12 = (bf16[4096,256]{1,0:T(8,128)(2,1)}, bf16[4096,256]{1,0:T(8,128)(2,1)}, u32[]{:S(2)}, u32[]{:S(2)}) collective-permute-start(bf16[4096,256]{1,0:T(8,128)(2,1)} %gather_fusion), channel_id=1, source_target_pairs={{0,8},{8,0},{16,24},{24,16},{1,9},{9,1},{17,25},{25,17},{2,10},{10... | collective-permute-start | bytes 6291464 | tf_op jit(solution)/shard_map/ppermute | solution.py:122
  174.1 73.9 %collective-permute-start.13 = (bf16[4096,256]{1,0:T(8,128)(2,1)}, bf16[4096,256]{1,0:T(8,128)(2,1)}, u32[]{:S(2)}, u32[]{:S(2)}) collective-permute-start(bf16[4096,256]{1,0:T(8,128)(2,1)} %gather_fusion), channel_id=1, source_target_pairs={{0,16},{8,24},{16,0},{24,8},{1,17},{9,25},{17,1},{25,9},{2,18},{10... | collective-permute-start | bytes 6291464 | tf_op jit(solution)/shard_map/ppermute | solution.py:122
  188.1 1.5 collective-permute-start.8
  188.9 1.0 collective-permute-start.7
  189.6 5.6 %copy-start.11 = (bf16[512,128]{1,0:T(8,128)(2,1)}, bf16[512,128]{1,0:T(8,128)(2,1)S(1)}, u32[]{:S(2)}) copy-start(bf16[512,128]{1,0:T(8,128)(2,1)S(1)} %collective-permute-done.8) | copy-start | bytes 393220
  189.6 52.6 %collective-permute-start.16 = (bf16[4096,128]{1,0:T(8,128)(2,1)S(1)}, bf16[4096,128]{1,0:T(8,128)(2,1)S(1)}, u32[]{:S(2)}, u32[]{:S(2)}) collective-permute-start(bf16[4096,128]{1,0:T(8,128)(2,1)S(1)} %gather_fusion.1), channel_id=1, source_target_pairs={{0,8},{8,0},{16,24},{24,16},{1,9},{9,1},{17,25},{25,17},{2,10},{10... | collective-permute-start | bytes 3145736 | tf_op jit(solution)/shard_map/ppermute | solution.py:122
  189.9 5.3 %copy-start.13 = (bf16[512,128]{1,0:T(8,128)(2,1)}, bf16[512,128]{1,0:T(8,128)(2,1)S(1)}, u32[]{:S(2)}) copy-start(bf16[512,128]{1,0:T(8,128)(2,1)S(1)} %collective-permute-done.7) | copy-start | bytes 393220
  189.9 0.7 collective-permute-start.6
  190.6 4.6 %copy-start.15 = (bf16[512,128]{1,0:T(8,128)(2,1)}, bf16[512,128]{1,0:T(8,128)(2,1)S(1)}, u32[]{:S(2)}) copy-start(bf16[512,128]{1,0:T(8,128)(2,1)S(1)} %collective-permute-done.6) | copy-start | bytes 393220
  190.7 3.2 %collective-permute-start.9 = (bf16[4,512,128]{2,1,0:T(8,128)(2,1)S(1)}, bf16[4,512,128]{2,1,0:T(8,128)(2,1)S(1)}, u32[]{:S(2)}, u32[]{:S(2)}) collective-permute-start(bf16[4,512,128]{2,1,0:T(8,128)(2,1)S(1)} %pad_maximum_fusion.3), channel_id=1, source_target_pairs={{7,3},{15,11},{23,19},{31,27}} | collective-permute-start | bytes 1572872 | tf_op jit(solution)/shard_map/ppermute | solution.py:152
  191.4 52.3 %collective-permute-start.17 = (bf16[4096,128]{1,0:T(8,128)(2,1)S(1)}, bf16[4096,128]{1,0:T(8,128)(2,1)S(1)}, u32[]{:S(2)}, u32[]{:S(2)}) collective-permute-start(bf16[4096,128]{1,0:T(8,128)(2,1)S(1)} %gather_fusion.1), channel_id=1, source_target_pairs={{0,16},{8,24},{16,0},{24,8},{1,17},{9,25},{17,1},{25,9},{2,18},{10... | collective-permute-start | bytes 3145736 | tf_op jit(solution)/shard_map/ppermute | solution.py:122
  193.9 48.2 %copy-start.9 = (bf16[4,512,128]{2,1,0:T(8,128)(2,1)}, bf16[4,512,128]{2,1,0:T(8,128)(2,1)S(1)}, u32[]{:S(2)}) copy-start(bf16[4,512,128]{2,1,0:T(8,128)(2,1)S(1)} %collective-permute-done.9) | copy-start | bytes 1572868
  193.9 101.7 %collective-permute-start.4 = (bf16[4,512,256]{2,1,0:T(8,128)(2,1)}, bf16[4,512,256]{2,1,0:T(8,128)(2,1)}, u32[]{:S(2)}, u32[]{:S(2)}) collective-permute-start(bf16[4,512,256]{2,1,0:T(8,128)(2,1)} %fusion.15), channel_id=1, source_target_pairs={{7,5},{3,1},{15,13},{11,9},{23,21},{19,17},{31,29},{27,25}} | collective-permute-start | bytes 3145736 | tf_op jit(solution)/shard_map/ppermute | solution.py:152
  242.1 51.7 %collective-permute-start.10 = (bf16[4,512,128]{2,1,0:T(8,128)(2,1)}, bf16[4,512,128]{2,1,0:T(8,128)(2,1)}, u32[]{:S(2)}, u32[]{:S(2)}) collective-permute-start(bf16[4,512,128]{2,1,0:T(8,128)(2,1)} %fusion.14), channel_id=1, source_target_pairs={{7,5},{3,1},{15,13},{11,9},{23,21},{19,17},{31,29},{27,25}} | collective-permute-start | bytes 1572872 | tf_op jit(solution)/shard_map/ppermute | solution.py:152
  243.7 55.1 %collective-permute-start.18 = (bf16[2048,128]{1,0:T(8,128)(2,1)S(1)}, bf16[2048,128]{1,0:T(8,128)(2,1)S(1)}, u32[]{:S(2)}, u32[]{:S(2)}) collective-permute-start(bf16[2048,128]{1,0:T(8,128)(2,1)S(1)} %slice.41), channel_id=1, source_target_pairs={{0,16},{8,24},{16,0},{24,8},{1,17},{9,25},{17,1},{25,9},{2,18},{10... | collective-permute-start | bytes 1572872 | tf_op jit(solution)/shard_map/ppermute | solution.py:122
  245.3 49.2 %copy-start.10 = (bf16[4,512,128]{2,1,0:T(8,128)(2,1)S(1)}, bf16[4,512,128]{2,1,0:T(8,128)(2,1)}, u32[]{:S(2)}) copy-start(bf16[4,512,128]{2,1,0:T(8,128)(2,1)} %copy-done.9) | copy-start | bytes 1572868
  245.4 49.2 %copy-start.12 = (bf16[512,128]{1,0:T(8,128)(2,1)S(1)}, bf16[512,128]{1,0:T(8,128)(2,1)}, u32[]{:S(2)}) copy-start(bf16[512,128]{1,0:T(8,128)(2,1)} %copy-done.11) | copy-start | bytes 393220
  245.4 49.1 %copy-start.14 = (bf16[512,128]{1,0:T(8,128)(2,1)S(1)}, bf16[512,128]{1,0:T(8,128)(2,1)}, u32[]{:S(2)}) copy-start(bf16[512,128]{1,0:T(8,128)(2,1)} %copy-done.13) | copy-start | bytes 393220
  245.4 49.1 %copy-start.16 = (bf16[512,128]{1,0:T(8,128)(2,1)S(1)}, bf16[512,128]{1,0:T(8,128)(2,1)}, u32[]{:S(2)}) copy-start(bf16[512,128]{1,0:T(8,128)(2,1)} %copy-done.15) | copy-start | bytes 393220
  245.4 54.9 %collective-permute-start.19 = (bf16[2048,128]{1,0:T(8,128)(2,1)S(1)}, bf16[2048,128]{1,0:T(8,128)(2,1)S(1)}, u32[]{:S(2)}, u32[]{:S(2)}) collective-permute-start(bf16[2048,128]{1,0:T(8,128)(2,1)S(1)} %slice.42), channel_id=1, source_target_pairs={{0,8},{8,0},{16,24},{24,16},{1,9},{9,1},{17,25},{25,17},{2,10},{10... | collective-permute-start | bytes 1572872 | tf_op jit(solution)/shard_map/ppermute | solution.py:122
  248.0 49.0 %copy-start.2 = (bf16[512,256]{1,0:T(8,128)(2,1)S(1)}, bf16[512,256]{1,0:T(8,128)(2,1)}, u32[]{:S(2)}) copy-start(bf16[512,256]{1,0:T(8,128)(2,1)} %copy-done) | copy-start | bytes 786436
  248.0 49.0 %copy-start.5 = (bf16[512,256]{1,0:T(8,128)(2,1)S(1)}, bf16[512,256]{1,0:T(8,128)(2,1)}, u32[]{:S(2)}) copy-start(bf16[512,256]{1,0:T(8,128)(2,1)} %copy-done.3) | copy-start | bytes 786436
  248.0 49.0 %copy-start.8 = (bf16[512,256]{1,0:T(8,128)(2,1)S(1)}, bf16[512,256]{1,0:T(8,128)(2,1)}, u32[]{:S(2)}) copy-start(bf16[512,256]{1,0:T(8,128)(2,1)} %copy-done.6) | copy-start | bytes 786436
  248.0 52.5 %collective-permute-start.14 = (bf16[2048,256]{1,0:T(8,128)(2,1)S(1)}, bf16[2048,256]{1,0:T(8,128)(2,1)S(1)}, u32[]{:S(2)}, u32[]{:S(2)}) collective-permute-start(bf16[2048,256]{1,0:T(8,128)(2,1)S(1)} %slice.39), channel_id=1, source_target_pairs={{0,16},{8,24},{16,0},{24,8},{1,17},{9,25},{17,1},{25,9},{2,18},{10... | collective-permute-start | bytes 3145736 | tf_op jit(solution)/shard_map/ppermute | solution.py:122
  293.8 13.6 %collective-permute-start.15 = (bf16[2048,256]{1,0:T(8,128)(2,1)S(1)}, bf16[2048,256]{1,0:T(8,128)(2,1)S(1)}, u32[]{:S(2)}, u32[]{:S(2)}) collective-permute-start(bf16[2048,256]{1,0:T(8,128)(2,1)S(1)} %slice.40), channel_id=1, source_target_pairs={{0,8},{8,0},{16,24},{24,16},{1,9},{9,1},{17,25},{25,17},{2,10},{10... | collective-permute-start | bytes 3145736 | tf_op jit(solution)/shard_map/ppermute | solution.py:122
  295.7 4.7 %collective-permute-start.11 = (bf16[4,512,128]{2,1,0:T(8,128)(2,1)S(1)}, bf16[4,512,128]{2,1,0:T(8,128)(2,1)S(1)}, u32[]{:S(2)}, u32[]{:S(2)}) collective-permute-start(bf16[4,512,128]{2,1,0:T(8,128)(2,1)S(1)} %fusion.17), channel_id=1, source_target_pairs={{7,6},{5,4},{3,2},{1,0},{15,14},{13,12},{11,10},{9,8},{23,22},{21,... | collective-permute-start | bytes 1572872 | tf_op jit(solution)/shard_map/ppermute | solution.py:152
  298.8 10.1 %collective-permute-start.5 = (bf16[4,512,256]{2,1,0:T(8,128)(2,1)S(1)}, bf16[4,512,256]{2,1,0:T(8,128)(2,1)S(1)}, u32[]{:S(2)}, u32[]{:S(2)}) collective-permute-start(bf16[4,512,256]{2,1,0:T(8,128)(2,1)S(1)} %fusion.18), channel_id=1, source_target_pairs={{7,6},{5,4},{3,2},{1,0},{15,14},{13,12},{11,10},{9,8},{23,22},{21,... | collective-permute-start | bytes 3145736 | tf_op jit(solution)/shard_map/ppermute | solution.py:152
  (6 other events, 14.6 us)

commit v3 on v2

v3 whole, which is shorter than its diff:
```python
import functools

import jax
import jax.numpy as jnp
from jax import lax
from jax.experimental import pallas as pl
from jax.experimental.pallas import tpu as pltpu
from jax.sharding import PartitionSpec as P

SLAB_DEV = 512
PICK_ROWS = 768
VMEM_LIMIT = 48 * 1024 * 1024


def pick_kernel(classes, offset, index_ref, probs_ref, root_ref, jacobian_ref, out_ref, matrix_ref):
    count_rows, steps, capacity, width = out_ref.shape
    local_width, all_rows = jacobian_ref.shape
    spans = [
        slice(r * (all_rows // count_rows) + offset, r * (all_rows // count_rows) + offset + width)
        for r in range(count_rows)
    ]

    @pl.when(pl.program_id(0) == 0)
    def _():
        down = lax.broadcasted_iota(jnp.int32, (width, width), 0) // classes
        across = lax.broadcasted_iota(jnp.int32, (width, width), 1) // classes
        for r, span in enumerate(spans):
            exact = jnp.where(down == across, probs_ref[span], 0.0)
            for part in range(3):
                piece = exact.astype(jnp.bfloat16)
                matrix_ref[part, r] = piece
                exact = exact - piece.astype(jnp.float32)

    lanes = lax.broadcasted_iota(jnp.int32, (steps * capacity, local_width), 1)
    onehot = jnp.where(lanes == index_ref[...], 1.0, 0.0).astype(jnp.bfloat16)
    for r, span in enumerate(spans):
        values = jnp.dot(onehot, jacobian_ref[:, span], preferred_element_type=jnp.float32)
        short = values.astype(jnp.bfloat16)
        centre = jnp.dot(short, matrix_ref[2, r], preferred_element_type=jnp.float32)
        centre += jnp.dot(short, matrix_ref[1, r], preferred_element_type=jnp.float32)
        centre += jnp.dot(short, matrix_ref[0, r], preferred_element_type=jnp.float32)
        weighted = (root_ref[:, span] * (values - centre)).astype(jnp.bfloat16)
        for t in range(steps):
            out_ref[r, t] = weighted[t * capacity : (t + 1) * capacity]


def pick_rows(jacobian, probs, root, send_index, count_rows, offset, width):
    count_cols, capacity = send_index.shape
    local_width, all_rows = jacobian.shape
    steps = max(1, min(count_cols, PICK_ROWS // capacity))
    shape = (count_rows, count_cols, capacity, width)
    picks = count_cols * capacity
    return pl.pallas_call(
        functools.partial(pick_kernel, probs.shape[1], offset),
        grid=(count_cols // steps,),
        in_specs=[
            pl.BlockSpec((steps * capacity, 1), lambda t: (t, 0)),
            pl.BlockSpec((all_rows, 1), lambda t: (0, 0)),
            pl.BlockSpec((1, all_rows), lambda t: (0, 0)),
            pl.BlockSpec((local_width, all_rows), lambda t: (0, 0)),
        ],
        out_specs=pl.BlockSpec((count_rows, steps, capacity, width), lambda t: (0, t, 0, 0)),
        out_shape=jax.ShapeDtypeStruct(shape, jnp.bfloat16),
        scratch_shapes=[pltpu.VMEM((3, count_rows, width, width), jnp.bfloat16)],
        cost_estimate=pl.CostEstimate(
            flops=2 * picks * local_width * width * count_rows,
            bytes_accessed=2 * local_width * all_rows + 2 * picks * width * count_rows,
            transcendentals=0,
        ),
        compiler_params=pltpu.CompilerParams(vmem_limit_bytes=VMEM_LIMIT),
    )(send_index.reshape(-1, 1), probs.reshape(all_rows, 1), root.reshape(1, all_rows), jacobian)


def product_kernel(chunks, offset_ref, *refs):
    slabs, tiles, out_ref = refs[:chunks], refs[chunks:-1], refs[-1]
    count = slabs[0].shape[0]
    total = None
    for c, slab in enumerate(slabs):
        for d in range(count):
            part = lax.dot_general(
                slab[d],
                tiles[c * count + d][...],
                (((1,), (1,)), ((), ())),
                preferred_element_type=jnp.float32,
            )
            total = part if total is None else total + part
    rows = offset_ref[0] + lax.broadcasted_iota(jnp.int32, out_ref.shape, 0)
    columns = (
        offset_ref[1]
        + pl.program_id(0) * out_ref.shape[1]
        + lax.broadcasted_iota(jnp.int32, out_ref.shape, 1)
    )
    out_ref[...] = jnp.where(columns <= rows, total, 0.0)


def product(slabs, tiles, offsets, tile_width):
    block = 512
    return pl.pallas_call(
        functools.partial(product_kernel, len(slabs)),
        grid=(tile_width // block,),
        in_specs=[pl.BlockSpec(memory_space=pltpu.SMEM)]
        + [pl.BlockSpec(slab.shape, lambda i: (0, 0, 0)) for slab in slabs]
        + [pl.BlockSpec((block, tile.shape[1]), lambda i: (i, 0)) for tile in tiles],
        out_specs=pl.BlockSpec((SLAB_DEV, block), lambda i: (0, i)),
        out_shape=jax.ShapeDtypeStruct((SLAB_DEV, tile_width), jnp.float32),
        compiler_params=pltpu.CompilerParams(vmem_limit_bytes=VMEM_LIMIT),
    )(offsets, *slabs, *tiles)


def exchange(x, count, d):
    return lax.ppermute(x, "gr", [(i, i ^ d) for i in range(count)])


def gather_pieces(block, count, gate):
    if count != 4:
        return [block] + [exchange(block, count, d) for d in range(1, count)], gate
    half = block.shape[0] // 2
    one, two = exchange(block, 4, 1), exchange(block, 4, 2)
    one, two, gate = lax.optimization_barrier((one, two, gate))
    top, bottom = exchange(one[:half], 4, 2), exchange(two[half:], 4, 1)
    return [block, one, two, jnp.concatenate([top, bottom])], gate


def collect_slab(block, count_rows, count_cols, grid_row, grid_col):
    first = block.shape[0] - SLAB_DEV * count_rows
    last = count_cols - 1

    def rows_of(r):
        return lax.dynamic_slice_in_dim(block, first + r * SLAB_DEV, SLAB_DEV, 0)

    own = rows_of(grid_row)
    parts = [jnp.where(grid_col == last, own, jnp.zeros_like(own))]
    for d in range(1, count_rows):
        pairs = [
            (r * count_cols + last, (r ^ d) * count_cols + last) for r in range(count_rows)
        ]
        parts.append(lax.ppermute(rows_of(grid_row ^ d), ("gr", "gc"), pairs))
    slab = jnp.stack(parts)
    return slab


def local(jacobian, class_scores, source):
    count_rows = lax.axis_size("gr")
    count_cols = lax.axis_size("gc")
    grid_row = lax.axis_index("gr")
    grid_col = lax.axis_index("gc")
    myself = grid_row * count_cols + grid_col
    local_width, all_rows = jacobian.shape
    total_weights = source.shape[0]
    tile_width = total_weights // count_cols
    capacity = 3 * (total_weights // (count_cols * count_cols * count_rows)) // 2
    block_rows = all_rows // count_rows
    widths = [block_rows]
    if block_rows % 384 == 0:
        widths = [2 * block_rows // 3, block_rows // 3]
    slab_total = SLAB_DEV * count_rows
    probs = class_scores / jnp.sum(class_scores, axis=1, keepdims=True)
    root = jnp.sqrt(probs)

    tiles = source.reshape(count_cols, tile_width)
    owned = tiles // local_width == myself
    rank = jnp.where(owned, jnp.cumsum(owned.astype(jnp.int32), axis=1) - 1, -1)
    slots = jnp.arange(capacity, dtype=jnp.int32)
    hit = rank[:, None, :] == slots[None, :, None]
    send_index = jnp.sum(jnp.where(hit, (tiles % local_width + 1)[:, None, :], 0), axis=2) - 1

    tile_source = (
        lax.dynamic_slice_in_dim(source, grid_col * tile_width, tile_width, 0) // local_width
    )
    lane_block = 128
    blocks = tile_source.reshape(-1, lane_block)
    place = jnp.arange(lane_block, dtype=jnp.int32)
    earlier = (blocks[:, :, None] == blocks[:, None, :]) & (place[None, :] < place[:, None])
    within = jnp.sum(earlier.astype(jnp.int32), axis=2)
    owner_ids = jnp.arange(count_rows * count_cols, dtype=jnp.int32)
    belongs = (blocks[:, None, :] == owner_ids[None, :, None]).astype(jnp.int32)
    counts = jnp.sum(belongs, axis=2)
    block_ids = jnp.arange(blocks.shape[0], dtype=jnp.int32)
    before = (block_ids[None, :] < block_ids[:, None]).astype(jnp.int32)
    base = jnp.sum(before[:, :, None] * counts[None, :, :], axis=1)
    arrival = (within + jnp.sum(belongs * base[:, :, None], axis=1)).reshape(-1)
    flat_index = tile_source * capacity + arrival

    slab_list, tile_list = [], []
    offset = 0
    for width in widths:
        part = pick_rows(jacobian, probs, root, send_index, count_rows, offset, width)
        offset += width
        incoming = lax.all_to_all(
            part.reshape(-1, capacity, width), ("gr", "gc"), split_axis=0, concat_axis=0, tiled=True
        )
        block = incoming.reshape(-1, width).at[flat_index].get(mode="promise_in_bounds")
        slab_list.append(collect_slab(block, count_rows, count_cols, grid_row, grid_col))
        if len(slab_list) == len(widths):
            block, slab_list = lax.optimization_barrier((block, slab_list))
            slab_list = lax.psum(slab_list, "gc")
            pieces, slab_list = gather_pieces(block, count_rows, slab_list)
        else:
            pieces, _ = gather_pieces(block, count_rows, [])
        tile_list += pieces
    offsets = jnp.stack(
        [total_weights - slab_total + grid_row * SLAB_DEV, grid_col * tile_width]
    ).astype(jnp.int32)
    return product(slab_list, tile_list, offsets, tile_width)


def solution(mesh):
    in_specs = (P(("gr", "gc"), None), P(), P())
    out_specs = P("gr", "gc")
    return jax.shard_map(local, mesh=mesh, in_specs=in_specs, out_specs=out_specs, check_vma=False)
```

time: 326 us -> 319 us (0.979)
  blocking collectives: 79 us -> 0 us
  waiting for transfers between devices: 97.2 us -> 165 us
  other arithmetic: 41.5 us -> 20.4 us
  between operations: 0.58 us -> 13.7 us
  Pallas kernels: 44.6 us -> 54.5 us
    all_to_all x1 -> x0, blocking collectives: 79 us -> none  [local(): lax.all_to_all(part.reshape(-1, capacity, width), ('gr', 'gc'), split_axi...]
    psum x0 -> x1, waiting for transfers between devices: none -> 73.5 us  [local(): slab_list = lax.psum(slab_list, 'gc')]
    all_to_all x1 -> x2, waiting for transfers between devices: 0.01 us -> 66.7 us  [local(): lax.all_to_all(part.reshape(-1, capacity, width), ('gr', 'gc'), split_axi...]
    ppermute x12 -> x6, waiting for transfers between devices: 44.3 us -> 0.02 us  [collect_slab(): parts.append(lax.ppermute(rows_of(grid_row ^ d), ('gr', 'gc'), pairs))]
    ppermute x8, waiting for transfers between devices: 52.9 us -> 24.6 us  [exchange(): return lax.ppermute(x, 'gr', [(i, i ^ d) for i in range(count)])]
    another operation x9 -> x6, other arithmetic: 23.5 us -> 5.81 us  [the longest x4 3.31 us: collect_slab(): slab = jnp.stack(parts)]
    pallas_call x1 -> x2, Pallas kernels: 31.1 us -> 41 us  [pick_rows(): pl.pallas_call(functools.partial(pick_kernel, probs.shape[1], offset), gr...]
    ppermute x12 -> x6, starting transfers between devices: 12 us -> 4.04 us  [collect_slab(): parts.append(lax.ppermute(rows_of(grid_row ^ d), ('gr', 'gc'), pairs))]
  transfers between devices with their start and end apart: 21 -> 17, of which waited for: 3 -> 6; matrix products, arithmetic and copies ran while one was open for 21% -> 14% of each run, Pallas kernels for 0% -> 6%
where the time goes in v3:
time: 319 us; the launch traced here: 315 us
  waiting for transfers between devices  165 us (52%)
  Pallas kernels  54.5 us (17%)
  local copies, waits for them, and re-layouts  39 us (12%)
  starting transfers between devices  22.1 us (7%)
  other arithmetic  20.4 us (6%)
  between operations  13.7 us (4%)
    psum x1, waiting for transfers between devices, local(): slab_list = lax.psum(slab_list, 'gc')  73.5 us
    all_to_all x2, waiting for transfers between devices, local(): lax.all_to_all(part.reshape(-1, capacity, width), ('gr', 'gc'), split_axi...  66.7 us
    pallas_call x2, Pallas kernels, pick_rows(): pl.pallas_call(functools.partial(pick_kernel, probs.shape[1], offset), gr...  41 us
    gather x2, local copies, waits for them, and re-layouts, local(): incoming.reshape(-1, width).at[flat_index].get(mode='promise_in_bounds')  30.2 us
    ppermute x8, waiting for transfers between devices, exchange(): return lax.ppermute(x, 'gr', [(i, i ^ d) for i in range(count)])  24.6 us
    pallas_call x1, Pallas kernels, product(): pl.pallas_call(functools.partial(product_kernel, len(slabs)), grid=(tile_...  13.5 us
    all_to_all x2, starting transfers between devices, local(): lax.all_to_all(part.reshape(-1, capacity, width), ('gr', 'gc'), split_axi...  10.3 us
    ppermute x8, starting transfers between devices, exchange(): return lax.ppermute(x, 'gr', [(i, i ^ d) for i in range(count)])  7.72 us
  transfers between devices with their start and end apart: 17, of which 6 were waited for; matrix products, arithmetic and copies ran while one was open for 14% of the time, Pallas kernels for 6%

profile of v3, /device:TPU:1, one launch (start us, length us, event | category | flops | bytes accessed | tf_op | source)
XLA Modules:
  0.0 314.6 jit_solution(2696936155278133706)
XLA Ops:
  8.3 0.9 reshape.154
  9.3 1.0 fusion.6
  10.3 2.3 reduce-window.6
  13.3 3.6 %select_reduce_fusion = s32[8,192]{1,0:T(8,128)S(1)} fusion(s32[8,4096]{1,0:T(8,128)S(1)} %get-tuple-element.36, s32[8,4096]{1,0:T(8,128)S(1)} %get-tuple-element.35), kind=kLoop, calls=%fused_computation.2 | loop fusion | flops 18872832 | bytes 268288 | tf_op jit(solution)/shard_map/reduce_sum | solution.py:165
  17.8 21.8 %shard_map.38 = bf16[4,8,192,256]{3,2,1,0:T(8,128)(2,1)} custom-call(s32[1536,1]{1,0:T(8,128)S(1)} %sub.32.index_ref, f32[1536,1]{1,0:T(8,128)S(1)} %reshape.181.probs_ref, f32[1,1536]{1,0:T(1,128)S(1)} %reshape.158.root_ref, bf16[2048,1536]{1,0:T(8,128)(2,1)} %jacobian_ref.3), custom_call_target="tpu_custom_call" | custom-call | flops 6442450944 | bytes 9437184 | tf_op jit(solution)/shard_map/pallas_call | solution.py:53
  39.6 7.2 %all-to-all-start.1 = ((bf16[32,192,256]{2,1,0:T(8,128)(2,1)}), bf16[32,192,256]{2,1,0:T(8,128)(2,1)}, u32[]{:S(2)}, u32[]{:S(2)}) async-start(bf16[32,192,256]{2,1,0:T(8,128)(2,1)} %bitcast.7), calls=%async_computation.1 | async-start | bytes 6291456 | tf_op jit(solution)/shard_map/all_to_all | solution.py:189
  46.8 19.1 %shard_map.37 = bf16[4,8,192,128]{3,2,1,0:T(8,128)(2,1)} custom-call(s32[1536,1]{1,0:T(8,128)S(1)} %sub.32.index_ref, f32[1536,1]{1,0:T(8,128)S(1)} %reshape.181.probs_ref, f32[1,1536]{1,0:T(1,128)S(1)} %reshape.158.root_ref, bf16[2048,1536]{1,0:T(8,128)(2,1)} %jacobian_ref.3), custom_call_target="tpu_custom_call" | custom-call | flops 3221225472 | bytes 7864320 | tf_op jit(solution)/shard_map/pallas_call | solution.py:53
  65.9 53.0 %all-to-all-done.1 = bf16[32,192,256]{2,1,0:T(8,128)(2,1)} async-done(((bf16[32,192,256]{2,1,0:T(8,128)(2,1)}), bf16[32,192,256]{2,1,0:T(8,128)(2,1)}, u32[]{:S(2)}, u32[]{:S(2)}) %all-to-all-start.1) | async-done | bytes 3145760 | tf_op jit(solution)/shard_map/all_to_all | solution.py:189
  118.9 3.1 all-to-all-start
  123.9 1.3 convert_reduce_fusion
  126.0 18.1 %gather_fusion.1 = bf16[4096,256]{1,0:T(8,128)(2,1)} fusion(bf16[6144,256]{1,0:T(8,128)(2,1)} %bitcast.8, s32[4096]{0:T(1024)S(1)} %fusion.9), kind=kCustom, calls=%fused_computation.1 | custom fusion | bytes 4210688 | tf_op jit(solution)/shard_map/gather | solution.py:192
  144.1 1.4 collective-permute-start.8
  145.5 1.2 collective-permute-start.9
  146.7 13.8 %all-to-all-done = bf16[32,192,128]{2,1,0:T(8,128)(2,1)S(1)} async-done(((bf16[32,192,128]{2,1,0:T(8,128)(2,1)}), bf16[32,192,128]{2,1,0:T(8,128)(2,1)S(1)}, u32[]{:S(2)}, u32[]{:S(2)}) %all-to-all-start) | async-done | bytes 1572896 | tf_op jit(solution)/shard_map/all_to_all | solution.py:189
  160.5 12.1 %gather_fusion = bf16[4096,128]{1,0:T(8,128)(2,1)S(1)} fusion(bf16[6144,128]{1,0:T(8,128)(2,1)S(1)} %bitcast.28, s32[4096]{0:T(1024)S(1)} %fusion.9), kind=kCustom, calls=%fused_computation | custom fusion | bytes 2113536 | tf_op jit(solution)/shard_map/gather | solution.py:192
  174.7 1.3 select_bitcast_fusion
  178.0 0.9 pad_maximum_fusion.3
  178.9 1.1 pad_maximum_fusion.1
  180.0 1.0 collective-permute-start.7
  181.4 14.7 %collective-permute-done.8.refs_3_ = bf16[4096,256]{1,0:T(8,128)(2,1)} collective-permute-done((bf16[4096,256]{1,0:T(8,128)(2,1)}, bf16[4096,256]{1,0:T(8,128)(2,1)}, u32[]{:S(2)}, u32[]{:S(2)}) %collective-permute-start.8) | collective-permute-done | bytes 2097184 | tf_op jit(solution)/shard_map/ppermute | solution.py:111
  196.1 2.3 slice.20
  198.4 2.4 slice.21
  200.7 0.9 collective-permute-start.11
  202.2 73.5 %all-reduce.3.cloned.1.call-done = (bf16[4,512,256]{2,1,0:T(8,128)(2,1)}, bf16[4,512,128]{2,1,0:T(8,128)(2,1)}) async-done(((bf16[4,512,256]{2,1,0:T(8,128)(2,1)}, bf16[4,512,128]{2,1,0:T(8,128)(2,1)}), (bf16[4,512,256]{2,1,0:T(8,128)(2,1)}, bf16[4,512,128]{2,1,0:T(8,128)(2,1)})) %all-reduce.3.cloned.1.call-update) | async-done | bytes 1572880 | tf_op jit(solution)/shard_map/psum | solution.py:196
  275.8 0.9 slice.22
  276.6 0.8 slice.23
  277.5 1.1 collective-permute-start.13
  278.6 1.2 collective-permute-start.12
  279.8 9.1 %collective-permute-done.13 = bf16[2048,128]{1,0:T(8,128)(2,1)} collective-permute-done((bf16[2048,128]{1,0:T(8,128)(2,1)}, bf16[2048,128]{1,0:T(8,128)(2,1)}, u32[]{:S(2)}, u32[]{:S(2)}) %collective-permute-start.13) | collective-permute-done | bytes 524320 | tf_op jit(solution)/shard_map/ppermute | solution.py:111
  289.7 1.3 pad_maximum_fusion.2.refs_9_
  291.0 3.2 %pad_maximum_fusion.refs_5_ = bf16[4096,256]{1,0:T(8,128)(2,1)} fusion(bf16[2048,256]{1,0:T(8,128)(2,1)} %collective-permute-done.11, bf16[2048,256]{1,0:T(8,128)(2,1)} %collective-permute-done.10), kind=kLoop, calls=%fused_computation.4 | loop fusion | flops 4194304 | bytes 4194304 | tf_op jit(solution)/shard_map/concatenate | solution.py:121
  294.2 13.5 %shard_map.39 = f32[512,4096]{1,0:T(8,128)} custom-call(s32[2]{0:T(128)S(1)} %pad_add_fusion.offset_ref, bf16[4,512,256]{2,1,0:T(8,128)(2,1)S(1)} %copy-done, bf16[4,512,128]{2,1,0:T(8,128)(2,1)S(1)} %copy-done.1, bf16[4096,256]{1,0:T(8,128)(2,1)} %gather_fusion.1, bf16[4096,256]{1,0:T(8,128)(2,1)} %collective-permute-done.8.refs_3_, ...), custom_call_target="tpu_custom_call" | custom-call | tf_op jit(solution)/shard_map/pallas_call | solution.py:98
  (47 shorter events, 11.8 us)
Async XLA Ops:
  39.6 79.3 %all-to-all-start.1 = ((bf16[32,192,256]{2,1,0:T(8,128)(2,1)}), bf16[32,192,256]{2,1,0:T(8,128)(2,1)}, u32[]{:S(2)}, u32[]{:S(2)}) async-start(bf16[32,192,256]{2,1,0:T(8,128)(2,1)} %bitcast.7), calls=%async_computation.1 | async-start | bytes 6291456 | tf_op jit(solution)/shard_map/all_to_all | solution.py:189
  118.9 41.6 %all-to-all-start = ((bf16[32,192,128]{2,1,0:T(8,128)(2,1)}), bf16[32,192,128]{2,1,0:T(8,128)(2,1)S(1)}, u32[]{:S(2)}, u32[]{:S(2)}) async-start(bf16[32,192,128]{2,1,0:T(8,128)(2,1)} %bitcast.3), calls=%async_computation | async-start | bytes 3145728 | tf_op jit(solution)/shard_map/all_to_all | solution.py:189
  122.0 153.8 %all-reduce.3.cloned.1.call-start = ((), (), s32[]{:S(2)}) async-start(), calls=%async_computation.2 | async-start | bytes 3145728 | tf_op jit(solution)/shard_map/psum | solution.py:196
  144.1 52.0 %collective-permute-start.8 = (bf16[4096,256]{1,0:T(8,128)(2,1)}, bf16[4096,256]{1,0:T(8,128)(2,1)}, u32[]{:S(2)}, u32[]{:S(2)}) collective-permute-start(bf16[4096,256]{1,0:T(8,128)(2,1)} %gather_fusion.1), channel_id=1, source_target_pairs={{0,8},{8,0},{16,24},{24,16},{1,9},{9,1},{17,25},{25,17},{2,10},{10... | collective-permute-start | bytes 6291464 | tf_op jit(solution)/shard_map/ppermute | solution.py:111
  145.5 50.6 %collective-permute-start.9 = (bf16[4096,256]{1,0:T(8,128)(2,1)}, bf16[4096,256]{1,0:T(8,128)(2,1)}, u32[]{:S(2)}, u32[]{:S(2)}) collective-permute-start(bf16[4096,256]{1,0:T(8,128)(2,1)} %gather_fusion.1), channel_id=1, source_target_pairs={{0,16},{8,24},{16,0},{24,8},{1,17},{9,25},{17,1},{25,9},{2,18},{10... | collective-permute-start | bytes 6291464 | tf_op jit(solution)/shard_map/ppermute | solution.py:111
  172.7 3.3 %collective-permute-start.5 = (bf16[512,128]{1,0:T(8,128)(2,1)S(1)}, bf16[512,128]{1,0:T(8,128)(2,1)S(1)}, u32[]{:S(2)}, u32[]{:S(2)}) collective-permute-start(bf16[512,128]{1,0:T(8,128)(2,1)S(1)} %get-tuple-element.32), channel_id=1, source_target_pairs={{7,31},{15,23},{23,15},{31,7}} | collective-permute-start | bytes 393224 | tf_op jit(solution)/shard_map/ppermute | solution.py:137
  173.3 3.3 %collective-permute-start.4 = (bf16[512,128]{1,0:T(8,128)(2,1)S(1)}, bf16[512,128]{1,0:T(8,128)(2,1)S(1)}, u32[]{:S(2)}, u32[]{:S(2)}) collective-permute-start(bf16[512,128]{1,0:T(8,128)(2,1)S(1)} %get-tuple-element.33), channel_id=1, source_target_pairs={{7,23},{15,31},{23,7},{31,15}} | collective-permute-start | bytes 393224 | tf_op jit(solution)/shard_map/ppermute | solution.py:137
  174.0 3.3 %collective-permute-start.3 = (bf16[512,128]{1,0:T(8,128)(2,1)S(1)}, bf16[512,128]{1,0:T(8,128)(2,1)S(1)}, u32[]{:S(2)}, u32[]{:S(2)}) collective-permute-start(bf16[512,128]{1,0:T(8,128)(2,1)S(1)} %get-tuple-element.34), channel_id=1, source_target_pairs={{7,15},{15,7},{23,31},{31,23}} | collective-permute-start | bytes 393224 | tf_op jit(solution)/shard_map/ppermute | solution.py:137
  176.0 3.0 collective-permute-start.2
  176.7 2.3 collective-permute-start.1
  177.4 1.6 collective-permute-start
  180.0 95.7 %collective-permute-start.7 = (bf16[4096,128]{1,0:T(8,128)(2,1)S(1)}, bf16[4096,128]{1,0:T(8,128)(2,1)S(1)}, u32[]{:S(2)}, u32[]{:S(2)}) collective-permute-start(bf16[4096,128]{1,0:T(8,128)(2,1)S(1)} %gather_fusion), channel_id=1, source_target_pairs={{0,16},{8,24},{16,0},{24,8},{1,17},{9,25},{17,1},{25,9},{2,18},{10... | collective-permute-start | bytes 3145736 | tf_op jit(solution)/shard_map/ppermute | solution.py:111
  181.1 94.7 %collective-permute-start.6 = (bf16[4096,128]{1,0:T(8,128)(2,1)S(1)}, bf16[4096,128]{1,0:T(8,128)(2,1)S(1)}, u32[]{:S(2)}, u32[]{:S(2)}) collective-permute-start(bf16[4096,128]{1,0:T(8,128)(2,1)S(1)} %gather_fusion), channel_id=1, source_target_pairs={{0,8},{8,0},{16,24},{24,16},{1,9},{9,1},{17,25},{25,17},{2,10},{10... | collective-permute-start | bytes 3145736 | tf_op jit(solution)/shard_map/ppermute | solution.py:111
  200.7 90.3 %collective-permute-start.11 = (bf16[2048,256]{1,0:T(8,128)(2,1)}, bf16[2048,256]{1,0:T(8,128)(2,1)}, u32[]{:S(2)}, u32[]{:S(2)}) collective-permute-start(bf16[2048,256]{1,0:T(8,128)(2,1)} %slice.21), channel_id=1, source_target_pairs={{0,8},{8,0},{16,24},{24,16},{1,9},{9,1},{17,25},{25,17},{2,10},{10... | collective-permute-start | bytes 3145736 | tf_op jit(solution)/shard_map/ppermute | solution.py:111
  201.7 89.3 %collective-permute-start.10 = (bf16[2048,256]{1,0:T(8,128)(2,1)}, bf16[2048,256]{1,0:T(8,128)(2,1)}, u32[]{:S(2)}, u32[]{:S(2)}) collective-permute-start(bf16[2048,256]{1,0:T(8,128)(2,1)} %slice.20), channel_id=1, source_target_pairs={{0,16},{8,24},{16,0},{24,8},{1,17},{9,25},{17,1},{25,9},{2,18},{10... | collective-permute-start | bytes 3145736 | tf_op jit(solution)/shard_map/ppermute | solution.py:111
  277.5 11.5 %collective-permute-start.13 = (bf16[2048,128]{1,0:T(8,128)(2,1)}, bf16[2048,128]{1,0:T(8,128)(2,1)}, u32[]{:S(2)}, u32[]{:S(2)}) collective-permute-start(bf16[2048,128]{1,0:T(8,128)(2,1)} %slice.23), channel_id=1, source_target_pairs={{0,8},{8,0},{16,24},{24,16},{1,9},{9,1},{17,25},{25,17},{2,10},{10... | collective-permute-start | bytes 1572872 | tf_op jit(solution)/shard_map/ppermute | solution.py:111
  278.6 11.1 %collective-permute-start.12 = (bf16[2048,128]{1,0:T(8,128)(2,1)}, bf16[2048,128]{1,0:T(8,128)(2,1)}, u32[]{:S(2)}, u32[]{:S(2)}) collective-permute-start(bf16[2048,128]{1,0:T(8,128)(2,1)} %slice.22), channel_id=1, source_target_pairs={{0,16},{8,24},{16,0},{24,8},{1,17},{9,25},{17,1},{25,9},{2,18},{10... | collective-permute-start | bytes 1572872 | tf_op jit(solution)/shard_map/ppermute | solution.py:111
  291.0 3.2 %copy-start = (bf16[4,512,256]{2,1,0:T(8,128)(2,1)S(1)}, bf16[4,512,256]{2,1,0:T(8,128)(2,1)}, u32[]{:S(2)}) copy-start(bf16[4,512,256]{2,1,0:T(8,128)(2,1)} %get-tuple-element.17.refs_0_) | copy-start | bytes 3145732
  291.0 3.2 %copy-start.1 = (bf16[4,512,128]{2,1,0:T(8,128)(2,1)S(1)}, bf16[4,512,128]{2,1,0:T(8,128)(2,1)}, u32[]{:S(2)}) copy-start(bf16[4,512,128]{2,1,0:T(8,128)(2,1)} %get-tuple-element.18.refs_1_) | copy-start | bytes 1572868
Sparse Core Ops, SparseCore 0:
  181.5 94.2 all-reduce.2

commit v4 on v3

--- a/solution.py
+++ b/solution.py
@@ -190,10 +190,10 @@
             part.reshape(-1, capacity, width), ("gr", "gc"), split_axis=0, concat_axis=0, tiled=True
         )
         block = incoming.reshape(-1, width).at[flat_index].get(mode="promise_in_bounds")
-        slab_list.append(collect_slab(block, count_rows, count_cols, grid_row, grid_col))
+        slab = collect_slab(block, count_rows, count_cols, grid_row, grid_col)
+        block, slab, slab_list = lax.optimization_barrier((block, slab, slab_list))
+        slab_list.append(lax.psum(slab, "gc"))
         if len(slab_list) == len(widths):
-            block, slab_list = lax.optimization_barrier((block, slab_list))
-            slab_list = lax.psum(slab_list, "gc")
             pieces, slab_list = gather_pieces(block, count_rows, slab_list)
         else:
             pieces, _ = gather_pieces(block, count_rows, [])

time: 319 us -> 322 us (level)
    psum x1 -> x2, waiting for transfers between devices: 73.5 us -> 95.7 us  [local(): slab_list.append(lax.psum(slab, 'gc'))]
    ppermute x8, waiting for transfers between devices: 24.6 us -> 9.67 us  [exchange(): return lax.ppermute(x, 'gr', [(i, i ^ d) for i in range(count)])]
    all_to_all x2, waiting for transfers between devices: 66.7 us -> 62.2 us  [local(): lax.all_to_all(part.reshape(-1, capacity, width), ('gr', 'gc'), split_axi...]
  transfers between devices with their start and end apart: 17 -> 18, of which waited for: 6 -> 6; matrix products, arithmetic and copies ran while one was open for 14% -> 14% of each run, Pallas kernels for 6% -> 6%
where the time goes in v4:
time: 322 us; the launch traced here: 317 us
  waiting for transfers between devices  168 us (52%)
  Pallas kernels  54.5 us (17%)
  local copies, waits for them, and re-layouts  39 us (12%)
  starting transfers between devices  22.3 us (7%)
  other arithmetic  20.4 us (6%)
  between operations  13.7 us (4%)
    psum x2, waiting for transfers between devices, local(): slab_list.append(lax.psum(slab, 'gc'))  95.7 us
    all_to_all x2, waiting for transfers between devices, local(): lax.all_to_all(part.reshape(-1, capacity, width), ('gr', 'gc'), split_axi...  62.2 us
    pallas_call x2, Pallas kernels, pick_rows(): pl.pallas_call(functools.partial(pick_kernel, probs.shape[1], offset), gr...  41 us
    gather x2, local copies, waits for them, and re-layouts, local(): incoming.reshape(-1, width).at[flat_index].get(mode='promise_in_bounds')  30.2 us
    pallas_call x1, Pallas kernels, product(): pl.pallas_call(functools.partial(product_kernel, len(slabs)), grid=(tile_...  13.5 us
    all_to_all x2, starting transfers between devices, local(): lax.all_to_all(part.reshape(-1, capacity, width), ('gr', 'gc'), split_axi...  10.3 us
    ppermute x8, waiting for transfers between devices, exchange(): return lax.ppermute(x, 'gr', [(i, i ^ d) for i in range(count)])  9.67 us
    ppermute x8, starting transfers between devices, exchange(): return lax.ppermute(x, 'gr', [(i, i ^ d) for i in range(count)])  7.92 us
  transfers between devices with their start and end apart: 18, of which 6 were waited for; matrix products, arithmetic and copies ran while one was open for 14% of the time, Pallas kernels for 6%

profile of v4, /device:TPU:1, one launch (start us, length us, event | category | flops | bytes accessed | tf_op | source)
XLA Modules:
  0.0 317.5 jit_solution(62952046219140088)
XLA Ops:
  8.3 0.9 reshape.154
  9.3 1.0 fusion.6
  10.3 2.3 reduce-window.6
  13.3 3.5 %select_reduce_fusion = s32[8,192]{1,0:T(8,128)S(1)} fusion(s32[8,4096]{1,0:T(8,128)S(1)} %get-tuple-element.38, s32[8,4096]{1,0:T(8,128)S(1)} %get-tuple-element.37), kind=kLoop, calls=%fused_computation.2 | loop fusion | flops 18872832 | bytes 268288 | tf_op jit(solution)/shard_map/reduce_sum | solution.py:165
  17.7 21.8 %shard_map.38 = bf16[4,8,192,256]{3,2,1,0:T(8,128)(2,1)} custom-call(s32[1536,1]{1,0:T(8,128)S(1)} %sub.32.index_ref, f32[1536,1]{1,0:T(8,128)S(1)} %reshape.181.probs_ref, f32[1,1536]{1,0:T(1,128)S(1)} %reshape.158.root_ref, bf16[2048,1536]{1,0:T(8,128)(2,1)} %jacobian_ref.3), custom_call_target="tpu_custom_call" | custom-call | flops 6442450944 | bytes 9437184 | tf_op jit(solution)/shard_map/pallas_call | solution.py:53
  39.5 7.2 %all-to-all-start.1 = ((bf16[32,192,256]{2,1,0:T(8,128)(2,1)}), bf16[32,192,256]{2,1,0:T(8,128)(2,1)}, u32[]{:S(2)}, u32[]{:S(2)}) async-start(bf16[32,192,256]{2,1,0:T(8,128)(2,1)} %bitcast.11), calls=%async_computation.1 | async-start | bytes 6291456 | tf_op jit(solution)/shard_map/all_to_all | solution.py:189
  46.7 19.1 %shard_map.37 = bf16[4,8,192,128]{3,2,1,0:T(8,128)(2,1)} custom-call(s32[1536,1]{1,0:T(8,128)S(1)} %sub.32.index_ref, f32[1536,1]{1,0:T(8,128)S(1)} %reshape.181.probs_ref, f32[1,1536]{1,0:T(1,128)S(1)} %reshape.158.root_ref, bf16[2048,1536]{1,0:T(8,128)(2,1)} %jacobian_ref.3), custom_call_target="tpu_custom_call" | custom-call | flops 3221225472 | bytes 7864320 | tf_op jit(solution)/shard_map/pallas_call | solution.py:53
  65.8 53.0 %all-to-all-done.1 = bf16[32,192,256]{2,1,0:T(8,128)(2,1)} async-done(((bf16[32,192,256]{2,1,0:T(8,128)(2,1)}), bf16[32,192,256]{2,1,0:T(8,128)(2,1)}, u32[]{:S(2)}, u32[]{:S(2)}) %all-to-all-start.1) | async-done | bytes 3145760 | tf_op jit(solution)/shard_map/all_to_all | solution.py:189
  118.8 3.1 all-to-all-start
  123.8 1.3 convert_reduce_fusion
  125.9 18.1 %gather_fusion.1 = bf16[4096,256]{1,0:T(8,128)(2,1)} fusion(bf16[6144,256]{1,0:T(8,128)(2,1)} %bitcast.12, s32[4096]{0:T(1024)S(1)} %fusion.9), kind=kCustom, calls=%fused_computation.1 | custom fusion | bytes 4210688 | tf_op jit(solution)/shard_map/gather | solution.py:192
  144.0 1.3 select_bitcast_fusion
  147.4 1.1 pad_maximum_fusion.1
  148.5 1.4 collective-permute-start.9
  149.9 1.2 collective-permute-start.8
  151.1 9.2 %all-to-all-done = bf16[32,192,128]{2,1,0:T(8,128)(2,1)S(1)} async-done(((bf16[32,192,128]{2,1,0:T(8,128)(2,1)}), bf16[32,192,128]{2,1,0:T(8,128)(2,1)S(1)}, u32[]{:S(2)}, u32[]{:S(2)}) %all-to-all-start) | async-done | bytes 1572896 | tf_op jit(solution)/shard_map/all_to_all | solution.py:189
  160.4 12.1 %gather_fusion = bf16[4096,128]{1,0:T(8,128)(2,1)S(1)} fusion(bf16[6144,128]{1,0:T(8,128)(2,1)S(1)} %bitcast.28, s32[4096]{0:T(1024)S(1)} %fusion.9), kind=kCustom, calls=%fused_computation | custom fusion | bytes 2113536 | tf_op jit(solution)/shard_map/gather | solution.py:192
  174.6 0.9 pad_maximum_fusion.3
  175.5 45.7 %all-reduce.3.cloned.1.call-done.refs_0_ = bf16[4,512,256]{2,1,0:T(8,128)(2,1)} async-done(((bf16[4,512,256]{2,1,0:T(8,128)(2,1)}), bf16[4,512,256]{2,1,0:T(8,128)(2,1)}) %all-reduce.3.cloned.1.call-update) | async-done | bytes 1048592 | tf_op jit(solution)/shard_map/psum | solution.py:195
  221.3 1.2 collective-permute-start.7
  222.5 1.2 collective-permute-start.6
  223.7 2.3 slice.20
  226.0 2.3 slice.21
  228.8 50.0 %all-reduce.5.cloned.1.call-done.refs_1_ = bf16[4,512,128]{2,1,0:T(8,128)(2,1)} async-done(((bf16[4,512,128]{2,1,0:T(8,128)(2,1)}), bf16[4,512,128]{2,1,0:T(8,128)(2,1)}) %all-reduce.5.cloned.1.call-update) | async-done | bytes 524304 | tf_op jit(solution)/shard_map/psum | solution.py:195
  278.8 0.9 slice.22
  280.5 1.2 collective-permute-start.13
  281.7 1.2 collective-permute-start.12
  283.0 8.7 %collective-permute-done.13 = bf16[2048,128]{1,0:T(8,128)(2,1)} collective-permute-done((bf16[2048,128]{1,0:T(8,128)(2,1)}, bf16[2048,128]{1,0:T(8,128)(2,1)}, u32[]{:S(2)}, u32[]{:S(2)}) %collective-permute-start.13) | collective-permute-done | bytes 524320 | tf_op jit(solution)/shard_map/ppermute | solution.py:111
  291.7 0.9 collective-permute-done.12
  292.6 1.3 pad_maximum_fusion.2.refs_9_
  294.0 3.2 pad_maximum_fusion.refs_5_
  297.1 13.5 %shard_map.39 = f32[512,4096]{1,0:T(8,128)} custom-call(s32[2]{0:T(128)S(1)} %pad_add_fusion.offset_ref, bf16[4,512,256]{2,1,0:T(8,128)(2,1)S(1)} %copy-done, bf16[4,512,128]{2,1,0:T(8,128)(2,1)S(1)} %copy-done.1, bf16[4096,256]{1,0:T(8,128)(2,1)} %gather_fusion.1, bf16[4096,256]{1,0:T(8,128)(2,1)} %collective-permute-done.8.refs_3_, ...), custom_call_target="tpu_custom_call" | custom-call | tf_op jit(solution)/shard_map/pallas_call | solution.py:98
  (50 shorter events, 11.7 us)
Async XLA Ops:
  39.5 79.3 %all-to-all-start.1 = ((bf16[32,192,256]{2,1,0:T(8,128)(2,1)}), bf16[32,192,256]{2,1,0:T(8,128)(2,1)}, u32[]{:S(2)}, u32[]{:S(2)}) async-start(bf16[32,192,256]{2,1,0:T(8,128)(2,1)} %bitcast.11), calls=%async_computation.1 | async-start | bytes 6291456 | tf_op jit(solution)/shard_map/all_to_all | solution.py:189
  118.8 41.6 %all-to-all-start = ((bf16[32,192,128]{2,1,0:T(8,128)(2,1)}), bf16[32,192,128]{2,1,0:T(8,128)(2,1)S(1)}, u32[]{:S(2)}, u32[]{:S(2)}) async-start(bf16[32,192,128]{2,1,0:T(8,128)(2,1)} %bitcast.3), calls=%async_computation | async-start | bytes 3145728 | tf_op jit(solution)/shard_map/all_to_all | solution.py:189
  121.9 99.4 %all-reduce.3.cloned.1.call-start = ((), (), s32[]{:S(2)}) async-start(), calls=%async_computation.2 | async-start | bytes 2097152 | tf_op jit(solution)/shard_map/psum | solution.py:195
  145.3 2.1 collective-permute-start.5
  146.0 1.4 collective-permute-start.4
  146.6 0.7 collective-permute-start.3
  148.5 75.2 %collective-permute-start.9 = (bf16[4096,256]{1,0:T(8,128)(2,1)}, bf16[4096,256]{1,0:T(8,128)(2,1)}, u32[]{:S(2)}, u32[]{:S(2)}) collective-permute-start(bf16[4096,256]{1,0:T(8,128)(2,1)} %gather_fusion.1), channel_id=1, source_target_pairs={{0,16},{8,24},{16,0},{24,8},{1,17},{9,25},{17,1},{25,9},{2,18},{10... | collective-permute-start | bytes 6291464 | tf_op jit(solution)/shard_map/ppermute | solution.py:111
  149.9 73.8 %collective-permute-start.8 = (bf16[4096,256]{1,0:T(8,128)(2,1)}, bf16[4096,256]{1,0:T(8,128)(2,1)}, u32[]{:S(2)}, u32[]{:S(2)}) collective-permute-start(bf16[4096,256]{1,0:T(8,128)(2,1)} %gather_fusion.1), channel_id=1, source_target_pairs={{0,8},{8,0},{16,24},{24,16},{1,9},{9,1},{17,25},{25,17},{2,10},{10... | collective-permute-start | bytes 6291464 | tf_op jit(solution)/shard_map/ppermute | solution.py:111
  151.1 127.7 %all-reduce.5.cloned.1.call-start = ((), (), s32[]{:S(2)}) async-start(), calls=%async_computation.3 | async-start | bytes 1048576 | tf_op jit(solution)/shard_map/psum | solution.py:195
  172.6 2.0 collective-permute-start.2
  173.2 1.4 collective-permute-start.1
  173.9 0.7 collective-permute-start
  221.3 57.5 %collective-permute-start.7 = (bf16[4096,128]{1,0:T(8,128)(2,1)S(1)}, bf16[4096,128]{1,0:T(8,128)(2,1)S(1)}, u32[]{:S(2)}, u32[]{:S(2)}) collective-permute-start(bf16[4096,128]{1,0:T(8,128)(2,1)S(1)} %gather_fusion), channel_id=1, source_target_pairs={{0,16},{8,24},{16,0},{24,8},{1,17},{9,25},{17,1},{25,9},{2,18},{10... | collective-permute-start | bytes 3145736 | tf_op jit(solution)/shard_map/ppermute | solution.py:111
  222.5 56.3 %collective-permute-start.6 = (bf16[4096,128]{1,0:T(8,128)(2,1)S(1)}, bf16[4096,128]{1,0:T(8,128)(2,1)S(1)}, u32[]{:S(2)}, u32[]{:S(2)}) collective-permute-start(bf16[4096,128]{1,0:T(8,128)(2,1)S(1)} %gather_fusion), channel_id=1, source_target_pairs={{0,8},{8,0},{16,24},{24,16},{1,9},{9,1},{17,25},{25,17},{2,10},{10... | collective-permute-start | bytes 3145736 | tf_op jit(solution)/shard_map/ppermute | solution.py:111
  228.2 65.7 %collective-permute-start.11 = (bf16[2048,256]{1,0:T(8,128)(2,1)}, bf16[2048,256]{1,0:T(8,128)(2,1)}, u32[]{:S(2)}, u32[]{:S(2)}) collective-permute-start(bf16[2048,256]{1,0:T(8,128)(2,1)} %slice.21), channel_id=1, source_target_pairs={{0,8},{8,0},{16,24},{24,16},{1,9},{9,1},{17,25},{25,17},{2,10},{10... | collective-permute-start | bytes 3145736 | tf_op jit(solution)/shard_map/ppermute | solution.py:111
  228.5 65.4 %collective-permute-start.10 = (bf16[2048,256]{1,0:T(8,128)(2,1)}, bf16[2048,256]{1,0:T(8,128)(2,1)}, u32[]{:S(2)}, u32[]{:S(2)}) collective-permute-start(bf16[2048,256]{1,0:T(8,128)(2,1)} %slice.20), channel_id=1, source_target_pairs={{0,16},{8,24},{16,0},{24,8},{1,17},{9,25},{17,1},{25,9},{2,18},{10... | collective-permute-start | bytes 3145736 | tf_op jit(solution)/shard_map/ppermute | solution.py:111
  280.5 11.2 %collective-permute-start.13 = (bf16[2048,128]{1,0:T(8,128)(2,1)}, bf16[2048,128]{1,0:T(8,128)(2,1)}, u32[]{:S(2)}, u32[]{:S(2)}) collective-permute-start(bf16[2048,128]{1,0:T(8,128)(2,1)} %slice.23), channel_id=1, source_target_pairs={{0,8},{8,0},{16,24},{24,16},{1,9},{9,1},{17,25},{25,17},{2,10},{10... | collective-permute-start | bytes 1572872 | tf_op jit(solution)/shard_map/ppermute | solution.py:111
  281.7 10.9 %collective-permute-start.12 = (bf16[2048,128]{1,0:T(8,128)(2,1)}, bf16[2048,128]{1,0:T(8,128)(2,1)}, u32[]{:S(2)}, u32[]{:S(2)}) collective-permute-start(bf16[2048,128]{1,0:T(8,128)(2,1)} %slice.22), channel_id=1, source_target_pairs={{0,16},{8,24},{16,0},{24,8},{1,17},{9,25},{17,1},{25,9},{2,18},{10... | collective-permute-start | bytes 1572872 | tf_op jit(solution)/shard_map/ppermute | solution.py:111
  293.9 3.2 %copy-start = (bf16[4,512,256]{2,1,0:T(8,128)(2,1)S(1)}, bf16[4,512,256]{2,1,0:T(8,128)(2,1)}, u32[]{:S(2)}) copy-start(bf16[4,512,256]{2,1,0:T(8,128)(2,1)} %all-reduce.3.cloned.1.call-done.refs_0_) | copy-start | bytes 3145732
  293.9 3.2 %copy-start.1 = (bf16[4,512,128]{2,1,0:T(8,128)(2,1)S(1)}, bf16[4,512,128]{2,1,0:T(8,128)(2,1)}, u32[]{:S(2)}) copy-start(bf16[4,512,128]{2,1,0:T(8,128)(2,1)} %all-reduce.5.cloned.1.call-done.refs_1_) | copy-start | bytes 1572868
Sparse Core Ops, SparseCore 0:
  151.2 70.0 all-reduce.2
  223.8 54.9 all-reduce.4

commit v5 on v3

--- a/solution.py
+++ b/solution.py
@@ -139,6 +139,15 @@
     return slab
 
 
+def double_slab(slab, count_cols):
+    stride = count_cols // 2
+    while stride:
+        pairs = [(c, c - stride) for c in range(count_cols - 1, 0, -2 * stride)]
+        slab = slab + lax.ppermute(slab, "gc", pairs)
+        stride //= 2
+    return slab
+
+
 def local(jacobian, class_scores, source):
     count_rows = lax.axis_size("gr")
     count_cols = lax.axis_size("gc")
@@ -193,8 +202,8 @@
         slab_list.append(collect_slab(block, count_rows, count_cols, grid_row, grid_col))
         if len(slab_list) == len(widths):
             block, slab_list = lax.optimization_barrier((block, slab_list))
-            slab_list = lax.psum(slab_list, "gc")
-            pieces, slab_list = gather_pieces(block, count_rows, slab_list)
+            slab_list = [double_slab(slab, count_cols) for slab in slab_list]
+            pieces, _ = gather_pieces(block, count_rows, [])
         else:
             pieces, _ = gather_pieces(block, count_rows, [])
         tile_list += pieces

time: 319 us -> 303 us (0.950)
  between operations: 13.7 us -> 0.4 us
  waiting for transfers between devices: 165 us -> 152 us
  starting transfers between devices: 22.1 us -> 32.7 us
    psum x1 -> x0, waiting for transfers between devices: 73.5 us -> none  [local(): slab_list = lax.psum(slab_list, 'gc')]
    ppermute x0 -> x6, waiting for transfers between devices: none -> 37.1 us  [double_slab(): slab = slab + lax.ppermute(slab, 'gc', pairs)]
    ppermute x8, waiting for transfers between devices: 24.6 us -> 42.5 us  [exchange(): return lax.ppermute(x, 'gr', [(i, i ^ d) for i in range(count)])]
    ppermute x0 -> x6, starting transfers between devices: none -> 13.1 us  [double_slab(): slab = slab + lax.ppermute(slab, 'gc', pairs)]
    all_to_all x2, waiting for transfers between devices: 66.7 us -> 71.9 us  [local(): lax.all_to_all(part.reshape(-1, capacity, width), ('gr', 'gc'), split_axi...]
    add x0 -> x6, other arithmetic: none -> 4.74 us  [double_slab(): slab = slab + lax.ppermute(slab, 'gc', pairs)]
  transfers between devices with their start and end apart: 17 -> 22, of which waited for: 6 -> 7; matrix products, arithmetic and copies ran while one was open for 14% -> 16% of each run, Pallas kernels for 6% -> 7%
where the time goes in v5:
time: 303 us; the launch traced here: 300 us
  waiting for transfers between devices  152 us (50%)
  Pallas kernels  54.5 us (18%)
  local copies, waits for them, and re-layouts  37.6 us (12%)
  starting transfers between devices  32.7 us (11%)
  other arithmetic  23.3 us (8%)
    all_to_all x2, waiting for transfers between devices, local(): lax.all_to_all(part.reshape(-1, capacity, width), ('gr', 'gc'), split_axi...  71.9 us
    ppermute x8, waiting for transfers between devices, exchange(): return lax.ppermute(x, 'gr', [(i, i ^ d) for i in range(count)])  42.5 us
    pallas_call x2, Pallas kernels, pick_rows(): pl.pallas_call(functools.partial(pick_kernel, probs.shape[1], offset), gr...  40.9 us
    ppermute x6, waiting for transfers between devices, double_slab(): slab = slab + lax.ppermute(slab, 'gc', pairs)  37.1 us
    gather x2, local copies, waits for them, and re-layouts, local(): incoming.reshape(-1, width).at[flat_index].get(mode='promise_in_bounds')  30.3 us
    pallas_call x1, Pallas kernels, product(): pl.pallas_call(functools.partial(product_kernel, len(slabs)), grid=(tile_...  13.5 us
    ppermute x6, starting transfers between devices, double_slab(): slab = slab + lax.ppermute(slab, 'gc', pairs)  13.1 us
    all_to_all x2, starting transfers between devices, local(): lax.all_to_all(part.reshape(-1, capacity, width), ('gr', 'gc'), split_axi...  11 us
  transfers between devices with their start and end apart: 22, of which 7 were waited for; matrix products, arithmetic and copies ran while one was open for 16% of the time, Pallas kernels for 7%

profile of v5, /device:TPU:1, one launch (start us, length us, event | category | flops | bytes accessed | tf_op | source)
XLA Modules:
  0.0 300.0 jit_solution(14852386397287600781)
XLA Ops:
  2.7 1.0 fusion.6
  3.7 2.3 reduce-window.6
  6.8 3.6 %select_reduce_fusion = s32[8,192]{1,0:T(8,128)S(1)} fusion(s32[8,4096]{1,0:T(8,128)S(1)} %get-tuple-element.30, s32[8,4096]{1,0:T(8,128)S(1)} %get-tuple-element.29), kind=kLoop, calls=%fused_computation.2 | loop fusion | flops 18872832 | bytes 268288 | tf_op jit(solution)/shard_map/reduce_sum | solution.py:174
  11.3 19.1 %shard_map.37 = bf16[4,8,192,128]{3,2,1,0:T(8,128)(2,1)} custom-call(s32[1536,1]{1,0:T(8,128)S(1)} %sub.32.index_ref, f32[1536,1]{1,0:T(8,128)S(1)} %reshape.181.probs_ref, f32[1,1536]{1,0:T(1,128)S(1)} %reshape.158.root_ref, bf16[2048,1536]{1,0:T(8,128)(2,1)} %jacobian_ref.3), custom_call_target="tpu_custom_call" | custom-call | flops 3221225472 | bytes 7864320 | tf_op jit(solution)/shard_map/pallas_call | solution.py:53
  30.4 7.1 %all-to-all-start = ((bf16[32,192,128]{2,1,0:T(8,128)(2,1)}), bf16[32,192,128]{2,1,0:T(8,128)(2,1)S(1)}, u32[]{:S(2)}, u32[]{:S(2)}) async-start(bf16[32,192,128]{2,1,0:T(8,128)(2,1)} %bitcast.3), calls=%async_computation | async-start | bytes 3145728 | tf_op jit(solution)/shard_map/all_to_all | solution.py:198
  37.5 21.8 %shard_map.38 = bf16[4,8,192,256]{3,2,1,0:T(8,128)(2,1)} custom-call(s32[1536,1]{1,0:T(8,128)S(1)} %sub.32.index_ref, f32[1536,1]{1,0:T(8,128)S(1)} %reshape.181.probs_ref, f32[1,1536]{1,0:T(1,128)S(1)} %reshape.158.root_ref, bf16[2048,1536]{1,0:T(8,128)(2,1)} %jacobian_ref.3), custom_call_target="tpu_custom_call" | custom-call | flops 6442450944 | bytes 9437184 | tf_op jit(solution)/shard_map/pallas_call | solution.py:53
  59.3 16.4 %all-to-all-done = bf16[32,192,128]{2,1,0:T(8,128)(2,1)S(1)} async-done(((bf16[32,192,128]{2,1,0:T(8,128)(2,1)}), bf16[32,192,128]{2,1,0:T(8,128)(2,1)S(1)}, u32[]{:S(2)}, u32[]{:S(2)}) %all-to-all-start) | async-done | bytes 1572896 | tf_op jit(solution)/shard_map/all_to_all | solution.py:198
  75.7 3.9 %all-to-all-start.1 = ((bf16[32,192,256]{2,1,0:T(8,128)(2,1)}), bf16[32,192,256]{2,1,0:T(8,128)(2,1)}, u32[]{:S(2)}, u32[]{:S(2)}) async-start(bf16[32,192,256]{2,1,0:T(8,128)(2,1)} %bitcast.7), calls=%async_computation.1 | async-start | bytes 6291456 | tf_op jit(solution)/shard_map/all_to_all | solution.py:198
  81.5 1.3 convert_reduce_fusion
  83.6 12.1 %gather_fusion = bf16[4096,128]{1,0:T(8,128)(2,1)S(1)} fusion(bf16[6144,128]{1,0:T(8,128)(2,1)S(1)} %bitcast.28, s32[4096]{0:T(1024)S(1)} %fusion.9), kind=kCustom, calls=%fused_computation | custom fusion | bytes 2113536 | tf_op jit(solution)/shard_map/gather | solution.py:201
  96.5 55.5 %all-to-all-done.1 = bf16[32,192,256]{2,1,0:T(8,128)(2,1)} async-done(((bf16[32,192,256]{2,1,0:T(8,128)(2,1)}), bf16[32,192,256]{2,1,0:T(8,128)(2,1)}, u32[]{:S(2)}, u32[]{:S(2)}) %all-to-all-start.1) | async-done | bytes 3145760 | tf_op jit(solution)/shard_map/all_to_all | solution.py:198
  151.9 18.1 %gather_fusion.1 = bf16[4096,256]{1,0:T(8,128)(2,1)} fusion(bf16[6144,256]{1,0:T(8,128)(2,1)} %bitcast.8, s32[4096]{0:T(1024)S(1)} %fusion.9), kind=kCustom, calls=%fused_computation.1 | custom fusion | bytes 4210688 | tf_op jit(solution)/shard_map/gather | solution.py:201
  170.1 1.3 select_bitcast_fusion
  174.8 1.2 collective-permute-start.12
  178.1 1.3 collective-permute-start.10
  179.4 1.3 collective-permute-start.17
  181.3 37.1 %collective-permute-done.10 = bf16[4,512,128]{2,1,0:T(8,128)(2,1)S(1)} collective-permute-done((bf16[4,512,128]{2,1,0:T(8,128)(2,1)S(1)}, bf16[4,512,128]{2,1,0:T(8,128)(2,1)S(1)}, u32[]{:S(2)}, u32[]{:S(2)}) %collective-permute-start.10) | collective-permute-done | bytes 524320 | tf_op jit(solution)/shard_map/ppermute | solution.py:146
  218.4 1.3 collective-permute-start.7
  220.6 1.3 collective-permute-done.12.refs_3_
  221.8 5.4 %collective-permute-start.11 = (bf16[4,512,128]{2,1,0:T(8,128)(2,1)}, bf16[4,512,128]{2,1,0:T(8,128)(2,1)}, u32[]{:S(2)}, u32[]{:S(2)}) collective-permute-start(bf16[4,512,128]{2,1,0:T(8,128)(2,1)} %add.137), channel_id=1, source_target_pairs={{7,6},{5,4},{3,2},{1,0},{15,14},{13,12},{11,10},{9,8},{23,22},{21,... | collective-permute-start | bytes 1572872 | tf_op jit(solution)/shard_map/ppermute | solution.py:146
  227.2 1.2 slice.20
  228.4 1.1 slice.21
  229.6 16.6 %collective-permute-done.17.refs_8_ = bf16[4096,128]{1,0:T(8,128)(2,1)S(1)} collective-permute-done((bf16[4096,128]{1,0:T(8,128)(2,1)S(1)}, bf16[4096,128]{1,0:T(8,128)(2,1)S(1)}, u32[]{:S(2)}, u32[]{:S(2)}) %collective-permute-start.17) | collective-permute-done | bytes 1048608 | tf_op jit(solution)/shard_map/ppermute | solution.py:111
  249.3 1.0 collective-permute-start.18
  250.3 1.8 add.134
  252.1 3.7 %collective-permute-start.8 = (bf16[4,512,256]{2,1,0:T(8,128)(2,1)S(1)}, bf16[4,512,256]{2,1,0:T(8,128)(2,1)S(1)}, u32[]{:S(2)}, u32[]{:S(2)}) collective-permute-start(bf16[4,512,256]{2,1,0:T(8,128)(2,1)S(1)} %add.134), channel_id=1, source_target_pairs={{7,6},{5,4},{3,2},{1,0},{15,14},{13,12},{11,10},{9,8},{23,22},{21,... | collective-permute-start | bytes 3145736 | tf_op jit(solution)/shard_map/ppermute | solution.py:146
  255.9 1.3 add.138.refs_1_
  257.3 20.6 %collective-permute-done.19 = bf16[2048,128]{1,0:T(8,128)(2,1)} collective-permute-done((bf16[2048,128]{1,0:T(8,128)(2,1)}, bf16[2048,128]{1,0:T(8,128)(2,1)}, u32[]{:S(2)}, u32[]{:S(2)}) %collective-permute-start.19) | collective-permute-done | bytes 524320 | tf_op jit(solution)/shard_map/ppermute | solution.py:111
  277.9 4.0 %collective-permute-done.18 = bf16[2048,128]{1,0:T(8,128)(2,1)} collective-permute-done((bf16[2048,128]{1,0:T(8,128)(2,1)}, bf16[2048,128]{1,0:T(8,128)(2,1)}, u32[]{:S(2)}, u32[]{:S(2)}) %collective-permute-start.18) | collective-permute-done | bytes 524320 | tf_op jit(solution)/shard_map/ppermute | solution.py:111
  281.9 1.3 pad_maximum_fusion.2.refs_9_
  283.1 3.1 %pad_maximum_fusion.refs_5_ = bf16[4096,256]{1,0:T(8,128)(2,1)} fusion(bf16[2048,256]{1,0:T(8,128)(2,1)} %collective-permute-done.15, bf16[2048,256]{1,0:T(8,128)(2,1)} %collective-permute-done.14), kind=kLoop, calls=%fused_computation.4 | loop fusion | flops 4194304 | bytes 4194304 | tf_op jit(solution)/shard_map/concatenate | solution.py:121
  286.5 13.5 %shard_map.39 = f32[512,4096]{1,0:T(8,128)} custom-call(s32[2]{0:T(128)S(1)} %pad_add_fusion.offset_ref, bf16[4,512,256]{2,1,0:T(8,128)(2,1)S(1)} %add.135.refs_0_, bf16[4,512,128]{2,1,0:T(8,128)(2,1)S(1)} %add.138.refs_1_, bf16[4096,256]{1,0:T(8,128)(2,1)} %gather_fusion.1, bf16[4096,256]{1,0:T(8,128)(2,1)} %copy-done, bf16[4096,256]{1,0:T(8,128)(2,1)} %copy-done.1, ...), custom_call_target="tpu_custom_call" | custom-call | tf_op jit(solution)/shard_map/pallas_call | solution.py:98
  (66 shorter events, 18.1 us)
Async XLA Ops:
  30.4 45.4 %all-to-all-start = ((bf16[32,192,128]{2,1,0:T(8,128)(2,1)}), bf16[32,192,128]{2,1,0:T(8,128)(2,1)S(1)}, u32[]{:S(2)}, u32[]{:S(2)}) async-start(bf16[32,192,128]{2,1,0:T(8,128)(2,1)} %bitcast.3), calls=%async_computation | async-start | bytes 3145728 | tf_op jit(solution)/shard_map/all_to_all | solution.py:198
  75.7 76.2 %all-to-all-start.1 = ((bf16[32,192,256]{2,1,0:T(8,128)(2,1)}), bf16[32,192,256]{2,1,0:T(8,128)(2,1)}, u32[]{:S(2)}, u32[]{:S(2)}) async-start(bf16[32,192,256]{2,1,0:T(8,128)(2,1)} %bitcast.7), calls=%async_computation.1 | async-start | bytes 6291456 | tf_op jit(solution)/shard_map/all_to_all | solution.py:198
  95.8 78.3 %collective-permute-start.5 = (bf16[512,128]{1,0:T(8,128)(2,1)S(1)}, bf16[512,128]{1,0:T(8,128)(2,1)S(1)}, u32[]{:S(2)}, u32[]{:S(2)}) collective-permute-start(bf16[512,128]{1,0:T(8,128)(2,1)S(1)} %get-tuple-element.26), channel_id=1, source_target_pairs={{7,31},{15,23},{23,15},{31,7}} | collective-permute-start | bytes 393224 | tf_op jit(solution)/shard_map/ppermute | solution.py:137
  171.3 5.0 %collective-permute-start.2 = (bf16[512,256]{1,0:T(8,128)(2,1)S(1)}, bf16[512,256]{1,0:T(8,128)(2,1)S(1)}, u32[]{:S(2)}, u32[]{:S(2)}) collective-permute-start(bf16[512,256]{1,0:T(8,128)(2,1)S(1)} %get-tuple-element.22), channel_id=1, source_target_pairs={{7,31},{15,23},{23,15},{31,7}} | collective-permute-start | bytes 786440 | tf_op jit(solution)/shard_map/ppermute | solution.py:137
  172.0 4.3 %collective-permute-start.1 = (bf16[512,256]{1,0:T(8,128)(2,1)S(1)}, bf16[512,256]{1,0:T(8,128)(2,1)S(1)}, u32[]{:S(2)}, u32[]{:S(2)}) collective-permute-start(bf16[512,256]{1,0:T(8,128)(2,1)S(1)} %get-tuple-element.23), channel_id=1, source_target_pairs={{7,23},{15,31},{23,7},{31,15}} | collective-permute-start | bytes 786440 | tf_op jit(solution)/shard_map/ppermute | solution.py:137
  172.7 3.6 %collective-permute-start = (bf16[512,256]{1,0:T(8,128)(2,1)S(1)}, bf16[512,256]{1,0:T(8,128)(2,1)S(1)}, u32[]{:S(2)}, u32[]{:S(2)}) collective-permute-start(bf16[512,256]{1,0:T(8,128)(2,1)S(1)} %get-tuple-element.24), channel_id=1, source_target_pairs={{7,15},{15,7},{23,31},{31,23}} | collective-permute-start | bytes 786440 | tf_op jit(solution)/shard_map/ppermute | solution.py:137
  173.4 1.4 collective-permute-start.4
  174.1 0.7 collective-permute-start.3
  174.8 47.0 %collective-permute-start.12 = (bf16[4096,256]{1,0:T(8,128)(2,1)}, bf16[4096,256]{1,0:T(8,128)(2,1)S(1)}, u32[]{:S(2)}, u32[]{:S(2)}) collective-permute-start(bf16[4096,256]{1,0:T(8,128)(2,1)} %gather_fusion.1), channel_id=1, source_target_pairs={{0,8},{8,0},{16,24},{24,16},{1,9},{9,1},{17,25},{25,17},{2,10},{10... | collective-permute-start | bytes 6291464 | tf_op jit(solution)/shard_map/ppermute | solution.py:111
  176.1 51.1 %collective-permute-start.13 = (bf16[4096,256]{1,0:T(8,128)(2,1)}, bf16[4096,256]{1,0:T(8,128)(2,1)S(1)}, u32[]{:S(2)}, u32[]{:S(2)}) collective-permute-start(bf16[4096,256]{1,0:T(8,128)(2,1)} %gather_fusion.1), channel_id=1, source_target_pairs={{0,16},{8,24},{16,0},{24,8},{1,17},{9,25},{17,1},{25,9},{2,18},{10... | collective-permute-start | bytes 6291464 | tf_op jit(solution)/shard_map/ppermute | solution.py:111
  176.5 4.2 %collective-permute-start.6 = (bf16[4,512,256]{2,1,0:T(8,128)(2,1)S(1)}, bf16[4,512,256]{2,1,0:T(8,128)(2,1)S(1)}, u32[]{:S(2)}, u32[]{:S(2)}) collective-permute-start(bf16[4,512,256]{2,1,0:T(8,128)(2,1)S(1)} %pad_maximum_fusion.1), channel_id=1, source_target_pairs={{7,3},{15,11},{23,19},{31,27}} | collective-permute-start | bytes 3145736 | tf_op jit(solution)/shard_map/ppermute | solution.py:146
  177.2 0.7 collective-permute-start.9
  178.1 40.3 %collective-permute-start.10 = (bf16[4,512,128]{2,1,0:T(8,128)(2,1)S(1)}, bf16[4,512,128]{2,1,0:T(8,128)(2,1)S(1)}, u32[]{:S(2)}, u32[]{:S(2)}) collective-permute-start(bf16[4,512,128]{2,1,0:T(8,128)(2,1)S(1)} %add.136), channel_id=1, source_target_pairs={{7,5},{3,1},{15,13},{11,9},{23,21},{19,17},{31,29},{27,25}} | collective-permute-start | bytes 1572872 | tf_op jit(solution)/shard_map/ppermute | solution.py:146
  179.4 66.8 %collective-permute-start.17 = (bf16[4096,128]{1,0:T(8,128)(2,1)S(1)}, bf16[4096,128]{1,0:T(8,128)(2,1)S(1)}, u32[]{:S(2)}, u32[]{:S(2)}) collective-permute-start(bf16[4096,128]{1,0:T(8,128)(2,1)S(1)} %gather_fusion), channel_id=1, source_target_pairs={{0,16},{8,24},{16,0},{24,8},{1,17},{9,25},{17,1},{25,9},{2,18},{10... | collective-permute-start | bytes 3145736 | tf_op jit(solution)/shard_map/ppermute | solution.py:111
  180.7 65.5 %collective-permute-start.16 = (bf16[4096,128]{1,0:T(8,128)(2,1)S(1)}, bf16[4096,128]{1,0:T(8,128)(2,1)S(1)}, u32[]{:S(2)}, u32[]{:S(2)}) collective-permute-start(bf16[4096,128]{1,0:T(8,128)(2,1)S(1)} %gather_fusion), channel_id=1, source_target_pairs={{0,8},{8,0},{16,24},{24,16},{1,9},{9,1},{17,25},{25,17},{2,10},{10... | collective-permute-start | bytes 3145736 | tf_op jit(solution)/shard_map/ppermute | solution.py:111
  181.2 48.2 %copy-start.2 = (bf16[4,512,256]{2,1,0:T(8,128)(2,1)}, bf16[4,512,256]{2,1,0:T(8,128)(2,1)S(1)}, u32[]{:S(2)}) copy-start(bf16[4,512,256]{2,1,0:T(8,128)(2,1)S(1)} %add.133) | copy-start | bytes 3145732
  218.4 30.0 %collective-permute-start.7 = (bf16[4,512,256]{2,1,0:T(8,128)(2,1)S(1)}, bf16[4,512,256]{2,1,0:T(8,128)(2,1)S(1)}, u32[]{:S(2)}, u32[]{:S(2)}) collective-permute-start(bf16[4,512,256]{2,1,0:T(8,128)(2,1)S(1)} %add.133), channel_id=1, source_target_pairs={{7,5},{3,1},{15,13},{11,9},{23,21},{19,17},{31,29},{27,25}} | collective-permute-start | bytes 3145736 | tf_op jit(solution)/shard_map/ppermute | solution.py:146
  221.8 7.6 %copy-start = (bf16[4096,256]{1,0:T(8,128)(2,1)}, bf16[4096,256]{1,0:T(8,128)(2,1)S(1)}, u32[]{:S(2)}) copy-start(bf16[4096,256]{1,0:T(8,128)(2,1)S(1)} %collective-permute-done.12.refs_3_) | copy-start | bytes 6291460
  221.8 30.3 %collective-permute-start.11 = (bf16[4,512,128]{2,1,0:T(8,128)(2,1)}, bf16[4,512,128]{2,1,0:T(8,128)(2,1)}, u32[]{:S(2)}, u32[]{:S(2)}) collective-permute-start(bf16[4,512,128]{2,1,0:T(8,128)(2,1)} %add.137), channel_id=1, source_target_pairs={{7,6},{5,4},{3,2},{1,0},{15,14},{13,12},{11,10},{9,8},{23,22},{21,... | collective-permute-start | bytes 1572872 | tf_op jit(solution)/shard_map/ppermute | solution.py:146
  227.2 2.3 copy-start.1
  229.5 53.6 %collective-permute-start.15 = (bf16[2048,256]{1,0:T(8,128)(2,1)}, bf16[2048,256]{1,0:T(8,128)(2,1)}, u32[]{:S(2)}, u32[]{:S(2)}) collective-permute-start(bf16[2048,256]{1,0:T(8,128)(2,1)} %slice.21), channel_id=1, source_target_pairs={{0,8},{8,0},{16,24},{24,16},{1,9},{9,1},{17,25},{25,17},{2,10},{10... | collective-permute-start | bytes 3145736 | tf_op jit(solution)/shard_map/ppermute | solution.py:111
  246.2 36.9 %collective-permute-start.14 = (bf16[2048,256]{1,0:T(8,128)(2,1)}, bf16[2048,256]{1,0:T(8,128)(2,1)}, u32[]{:S(2)}, u32[]{:S(2)}) collective-permute-start(bf16[2048,256]{1,0:T(8,128)(2,1)} %slice.20), channel_id=1, source_target_pairs={{0,16},{8,24},{16,0},{24,8},{1,17},{9,25},{17,1},{25,9},{2,18},{10... | collective-permute-start | bytes 3145736 | tf_op jit(solution)/shard_map/ppermute | solution.py:111
  247.9 30.0 %collective-permute-start.19 = (bf16[2048,128]{1,0:T(8,128)(2,1)}, bf16[2048,128]{1,0:T(8,128)(2,1)}, u32[]{:S(2)}, u32[]{:S(2)}) collective-permute-start(bf16[2048,128]{1,0:T(8,128)(2,1)} %slice.23), channel_id=1, source_target_pairs={{0,8},{8,0},{16,24},{24,16},{1,9},{9,1},{17,25},{25,17},{2,10},{10... | collective-permute-start | bytes 1572872 | tf_op jit(solution)/shard_map/ppermute | solution.py:111
  248.4 1.0 copy-start.3
  249.3 32.5 %collective-permute-start.18 = (bf16[2048,128]{1,0:T(8,128)(2,1)}, bf16[2048,128]{1,0:T(8,128)(2,1)}, u32[]{:S(2)}, u32[]{:S(2)}) collective-permute-start(bf16[2048,128]{1,0:T(8,128)(2,1)} %slice.22), channel_id=1, source_target_pairs={{0,16},{8,24},{16,0},{24,8},{1,17},{9,25},{17,1},{25,9},{2,18},{10... | collective-permute-start | bytes 1572872 | tf_op jit(solution)/shard_map/ppermute | solution.py:111
  252.1 34.1 %collective-permute-start.8 = (bf16[4,512,256]{2,1,0:T(8,128)(2,1)S(1)}, bf16[4,512,256]{2,1,0:T(8,128)(2,1)S(1)}, u32[]{:S(2)}, u32[]{:S(2)}) collective-permute-start(bf16[4,512,256]{2,1,0:T(8,128)(2,1)S(1)} %add.134), channel_id=1, source_target_pairs={{7,6},{5,4},{3,2},{1,0},{15,14},{13,12},{11,10},{9,8},{23,22},{21,... | collective-permute-start | bytes 3145736 | tf_op jit(solution)/shard_map/ppermute | solution.py:146
